TPU v7x, 32 devices: a whole 2x2x4 slice. The times are simulated.
32 devices in a mesh: dp: 4 (over y, x), row: 4 (over z), col: 2 (over core).
Axes of the slice: x: 2, y: 2, z: 4, core: 2. Of those that a mesh axis runs over, the one named last changes fastest.
Arguments:
- tokens: bfloat16 [16384, 1024], P(('dp', 'row'), 'col'), may hold values from -6 to 6
- segment: int32 [16, 1024], P(('dp', 'row')), may hold values from 0 to 3, never falling along the last dimension, each value on 1 to 512 neighbouring positions
- cotangent: bfloat16 [16384, 1024], P(('dp', 'row'), 'col'), may hold values from -6 to 6
- w_query: bfloat16 [1024, 1024], P('row', 'col'), may hold values from -0.1875 to 0.1875
- b_query: bfloat16 [1024], P('col'), may hold values from -2 to 2
- w_key: bfloat16 [1024, 1024], P('row', 'col'), may hold values from -0.1875 to 0.1875
- w_value: bfloat16 [1024, 1024], P('row', 'col'), may hold values from -0.1875 to 0.1875
- b_value: bfloat16 [1024], P('col'), may hold values from -2 to 2
- w_out: bfloat16 [1024, 1024], P('row', 'col'), may hold values from -1.5 to 1.5
- b_out: bfloat16 [1024], P('col'), may hold values from -2 to 2
- w_up: bfloat16 [1024, 4096], P('row', 'col'), may hold values from -0.1875 to 0.1875
- b_up: bfloat16 [4096], P('col'), may hold values from -2 to 2
- w_down: bfloat16 [4096, 1024], P('row', 'col'), may hold values from -0.09375 to 0.09375
- b_down: bfloat16 [1024], P('col'), may hold values from -2 to 2
- gain_one: bfloat16 [1024], P('col'), may hold values from 0.5 to 1.5
- shift_one: bfloat16 [1024], P('col'), may hold values from -2 to 2
- gain_two: bfloat16 [1024], P('col'), may hold values from 0.5 to 1.5
- shift_two: bfloat16 [1024], P('col'), may hold values from -2 to 2
Outputs:
- output: bfloat16 [16384, 1024], P(('dp', 'row'), 'col')
- d_tokens: bfloat16 [16384, 1024], P(('dp', 'row'), 'col')
- d_w_query: float32 [1024, 1024], P('row', 'col')
- d_b_query: float32 [1024], P('col')
- d_w_key: float32 [1024, 1024], P('row', 'col')
- d_w_value: float32 [1024, 1024], P('row', 'col')
- d_b_value: float32 [1024], P('col')
- d_w_out: float32 [1024, 1024], P('row', 'col')
- d_b_out: float32 [1024], P('col')
- d_w_up: float32 [1024, 4096], P('row', 'col')
- d_b_up: float32 [4096], P('col')
- d_w_down: float32 [4096, 1024], P('row', 'col')
- d_b_down: float32 [1024], P('col')
- d_gain_one: float32 [1024], P('col')
- d_shift_one: float32 [1024], P('col')
- d_gain_two: float32 [1024], P('col')
- d_shift_two: float32 [1024], P('col')
Inputs may be any that keep to these rules, and one draw needn't show every extreme that they name: `segment`: within each row (the 1024 tokens of one group) the numbers never fall; each number marks one sequence of 1 to 512 tokens, and some sequence has exactly 512.
All inputs are finite; a program needn't handle non-finite values.
Results may differ from a plain program's by a relative error of at most 0.018.
Values may be sent and summed in bfloat16 or wider, within the bound.
No kernel may reach another device: no remote copies, remote signals or barrier semaphores. Data moves between devices by JAX's collectives and lax.ppermute only.
A program may use at most 192 MiB of HBM per device.

v0:
```python
import jax
import jax.numpy as jnp
from jax import lax
from jax.sharding import PartitionSpec as P

HEAD_DIM = 64


EPSILON = 1e-05
SCALE = 0.125


def matmul(left, right):
    return jnp.dot(left, right, preferred_element_type=jnp.float32)


def matmul_tn(left, right):
    return lax.dot_general(
        left, right, (((0,), (0,)), ((), ())), preferred_element_type=jnp.float32
    )


def matmul_nt(left, right):
    return lax.dot_general(
        left, right, (((1,), (1,)), ((), ())), preferred_element_type=jnp.float32
    )


def whole_rows(part):
    return lax.all_gather(part, "col", axis=1, tiled=True)


def summed_rows(partial_value):
    return lax.psum_scatter(partial_value, "col", scatter_dimension=1, tiled=True)


def gelu_exact(values):
    return jax.nn.gelu(values, approximate=False)


def norm_forward(resid, gain, shift, width):
    first, second = lax.psum((jnp.sum(resid, axis=1), jnp.sum(resid * resid, axis=1)), "col")
    center = first / width
    inverse = lax.rsqrt(second / width - center * center + EPSILON)
    normed = (resid - center[:, None]) * inverse[:, None]
    return (normed * gain.astype(jnp.float32) + shift.astype(jnp.float32), normed, inverse)


def norm_backward(grad, normed, inverse, gain, width):
    scaled = grad * gain.astype(jnp.float32)
    first, second = lax.psum((jnp.sum(scaled, axis=1), jnp.sum(scaled * normed, axis=1)), "col")
    d_input = inverse[:, None] * (
        scaled - first[:, None] / width - normed * (second[:, None] / width)
    )
    return (d_input, jnp.sum(grad * normed, axis=0), jnp.sum(grad, axis=0))


def masked_scores(query_block, key_three, segment_ids, begin, block):
    raw = (
        jnp.einsum("qhd,khd->hqk", query_block, key_three, preferred_element_type=jnp.float32)
        * SCALE
    )
    same = segment_ids[begin : begin + block, None] == segment_ids[None, :]
    return jnp.where(same[None], raw, -1e30)


def attend(queries, key_rows, value_rows, segment_ids):
    count = queries.shape[0]
    heads_here = queries.shape[1] // HEAD_DIM
    block = min(512, count)
    query_three = queries.reshape(count, heads_here, HEAD_DIM)
    key_three = key_rows.reshape(count, heads_here, HEAD_DIM)
    value_three = value_rows.reshape(count, heads_here, HEAD_DIM)
    pieces = []
    totals = []
    for begin in range(0, count, block):
        scores = masked_scores(
            query_three[begin : begin + block], key_three, segment_ids, begin, block
        )
        row_top = jnp.max(scores, axis=2, keepdims=True)
        expo = jnp.exp(scores - row_top)
        total = jnp.sum(expo, axis=2, keepdims=True)
        probs = (expo / total).astype(jnp.bfloat16)
        pieces.append(
            jnp.einsum("hqk,khd->qhd", probs, value_three, preferred_element_type=jnp.float32)
        )
        totals.append((row_top + jnp.log(total))[:, :, 0])
    context = (
        jnp.concatenate(pieces, axis=0).reshape(count, heads_here * HEAD_DIM).astype(jnp.bfloat16)
    )
    return (context, jnp.concatenate(totals, axis=1))


def attend_back(queries, key_rows, value_rows, segment_ids, log_total, d_context):
    count = queries.shape[0]
    heads_here = queries.shape[1] // HEAD_DIM
    block = min(512, count)
    query_three = queries.reshape(count, heads_here, HEAD_DIM)
    key_three = key_rows.reshape(count, heads_here, HEAD_DIM)
    value_three = value_rows.reshape(count, heads_here, HEAD_DIM)
    grad_three = d_context.reshape(count, heads_here, HEAD_DIM)
    d_keys = jnp.zeros((count, heads_here, HEAD_DIM), jnp.float32)
    d_values = jnp.zeros((count, heads_here, HEAD_DIM), jnp.float32)
    pieces = []
    for begin in range(0, count, block):
        query_block = query_three[begin : begin + block]
        grad_block = grad_three[begin : begin + block]
        scores = masked_scores(query_block, key_three, segment_ids, begin, block)
        probs = jnp.exp(scores - log_total[:, begin : begin + block, None])
        d_probs = jnp.einsum(
            "qhd,khd->hqk", grad_block, value_three, preferred_element_type=jnp.float32
        )
        inner = jnp.sum(probs * d_probs, axis=2, keepdims=True)
        d_scores = (probs * (d_probs - inner)).astype(jnp.bfloat16)
        pieces.append(
            jnp.einsum("hqk,khd->qhd", d_scores, key_three, preferred_element_type=jnp.float32)
            * SCALE
        )
        d_keys = (
            d_keys
            + jnp.einsum("hqk,qhd->khd", d_scores, query_block, preferred_element_type=jnp.float32)
            * SCALE
        )
        d_values = d_values + jnp.einsum(
            "hqk,qhd->khd",
            probs.astype(jnp.bfloat16),
            grad_block,
            preferred_element_type=jnp.float32,
        )
    width = heads_here * HEAD_DIM
    d_queries = jnp.concatenate(pieces, axis=0).reshape(count, width).astype(jnp.bfloat16)
    return (
        d_queries,
        d_keys.reshape(count, width).astype(jnp.bfloat16),
        d_values.reshape(count, width).astype(jnp.bfloat16),
    )


def column_sum(values):
    return jnp.sum(values.astype(jnp.float32), axis=0)


def body(
    tokens,
    segment,
    cotangent,
    w_query,
    b_query,
    w_key,
    w_value,
    b_value,
    w_out,
    b_out,
    w_up,
    b_up,
    w_down,
    b_down,
    gain_one,
    shift_one,
    gain_two,
    shift_two,
):
    width = w_query.shape[1] * lax.axis_size("col")
    wq_full, wk_full, wv_full, wo_full, wu_full, wd_full = (
        lax.all_gather(w_query, "row", axis=0, tiled=True),
        lax.all_gather(w_key, "row", axis=0, tiled=True),
        lax.all_gather(w_value, "row", axis=0, tiled=True),
        lax.all_gather(w_out, "row", axis=0, tiled=True),
        lax.all_gather(w_up, "row", axis=0, tiled=True),
        lax.all_gather(w_down, "row", axis=0, tiled=True),
    )
    segment_ids = segment[0]
    token_rows = whole_rows(tokens)
    queries = (matmul(token_rows, wq_full) + b_query.astype(jnp.float32)).astype(jnp.bfloat16)
    key_rows = matmul(token_rows, wk_full).astype(jnp.bfloat16)
    value_rows = (matmul(token_rows, wv_full) + b_value.astype(jnp.float32)).astype(jnp.bfloat16)
    context, log_total = attend(queries, key_rows, value_rows, segment_ids)
    context_rows = whole_rows(context)
    branch = matmul(context_rows, wo_full) + b_out.astype(jnp.float32)
    normed_out, normed_one, inverse_one = norm_forward(
        tokens.astype(jnp.float32) + branch, gain_one, shift_one, width
    )
    hidden = normed_out.astype(jnp.bfloat16)
    hidden_rows = whole_rows(hidden)
    pre_act = matmul(hidden_rows, wu_full) + b_up.astype(jnp.float32)
    activated = lax.all_gather(gelu_exact(pre_act).astype(jnp.bfloat16), "col", axis=1, tiled=True)
    ffn_out = matmul(activated, wd_full) + b_down.astype(jnp.float32)
    final, normed_two, inverse_two = norm_forward(
        hidden.astype(jnp.float32) + ffn_out, gain_two, shift_two, width
    )
    output = final.astype(jnp.bfloat16)
    second_grad, d_gain_two, d_shift_two = norm_backward(
        cotangent.astype(jnp.float32), normed_two, inverse_two, gain_two, width
    )
    ffn_grad = second_grad.astype(jnp.bfloat16)
    d_w_down = matmul_tn(activated, ffn_grad)
    d_b_down = column_sum(ffn_grad)
    act_grad = lax.psum_scatter(
        matmul_nt(ffn_grad, wd_full), "col", scatter_dimension=1, tiled=True
    )
    pre_grad = jax.vjp(gelu_exact, pre_act)[1](act_grad)[0].astype(jnp.bfloat16)
    hidden_part = summed_rows(matmul_nt(pre_grad, wu_full))
    d_w_up = matmul_tn(hidden_rows, pre_grad)
    d_b_up = column_sum(pre_grad)
    first_grad, d_gain_one, d_shift_one = norm_backward(
        second_grad + hidden_part, normed_one, inverse_one, gain_one, width
    )
    branch_grad = first_grad.astype(jnp.bfloat16)
    d_w_out = matmul_tn(context_rows, branch_grad)
    d_b_out = column_sum(branch_grad)
    context_grad = summed_rows(matmul_nt(branch_grad, wo_full)).astype(jnp.bfloat16)
    query_grad, key_grad, value_grad = attend_back(
        queries, key_rows, value_rows, segment_ids, log_total, context_grad
    )
    d_w_query = matmul_tn(token_rows, query_grad)
    d_b_query = column_sum(query_grad)
    d_w_key = matmul_tn(token_rows, key_grad)
    d_w_value = matmul_tn(token_rows, value_grad)
    d_b_value = column_sum(value_grad)
    token_part = (
        matmul_nt(query_grad, wq_full)
        + matmul_nt(key_grad, wk_full)
        + matmul_nt(value_grad, wv_full)
    )
    d_tokens = (summed_rows(token_part) + first_grad).astype(jnp.bfloat16)
    rows_here = lax.axis_size("row")

    def tiled(vector):
        return jnp.broadcast_to(vector[None, :], (rows_here, vector.shape[0]))

    reduced = (
        lax.psum_scatter(
            d_w_query.astype(jnp.bfloat16), "row", scatter_dimension=0, tiled=True
        ).astype(jnp.float32),
        lax.psum_scatter(
            d_w_key.astype(jnp.bfloat16), "row", scatter_dimension=0, tiled=True
        ).astype(jnp.float32),
        lax.psum_scatter(
            d_w_value.astype(jnp.bfloat16), "row", scatter_dimension=0, tiled=True
        ).astype(jnp.float32),
        lax.psum_scatter(
            d_w_out.astype(jnp.bfloat16), "row", scatter_dimension=0, tiled=True
        ).astype(jnp.float32),
        lax.psum_scatter(
            d_w_up.astype(jnp.bfloat16), "row", scatter_dimension=0, tiled=True
        ).astype(jnp.float32),
        lax.psum_scatter(
            d_w_down.astype(jnp.bfloat16), "row", scatter_dimension=0, tiled=True
        ).astype(jnp.float32),
        lax.psum_scatter(
            tiled(d_b_query).astype(jnp.bfloat16), "row", scatter_dimension=0, tiled=True
        ).astype(jnp.float32),
        lax.psum_scatter(
            tiled(d_b_value).astype(jnp.bfloat16), "row", scatter_dimension=0, tiled=True
        ).astype(jnp.float32),
        lax.psum_scatter(
            tiled(d_b_out).astype(jnp.bfloat16), "row", scatter_dimension=0, tiled=True
        ).astype(jnp.float32),
        lax.psum_scatter(
            tiled(d_b_up).astype(jnp.bfloat16), "row", scatter_dimension=0, tiled=True
        ).astype(jnp.float32),
        lax.psum_scatter(
            tiled(d_b_down).astype(jnp.bfloat16), "row", scatter_dimension=0, tiled=True
        ).astype(jnp.float32),
        lax.psum_scatter(
            tiled(d_gain_one).astype(jnp.bfloat16), "row", scatter_dimension=0, tiled=True
        ).astype(jnp.float32),
        lax.psum_scatter(
            tiled(d_shift_one).astype(jnp.bfloat16), "row", scatter_dimension=0, tiled=True
        ).astype(jnp.float32),
        lax.psum_scatter(
            tiled(d_gain_two).astype(jnp.bfloat16), "row", scatter_dimension=0, tiled=True
        ).astype(jnp.float32),
        lax.psum_scatter(
            tiled(d_shift_two).astype(jnp.bfloat16), "row", scatter_dimension=0, tiled=True
        ).astype(jnp.float32),
    )
    summed = (
        lax.psum(reduced[0].astype(jnp.bfloat16), "dp").astype(jnp.float32),
        lax.psum(reduced[1].astype(jnp.bfloat16), "dp").astype(jnp.float32),
        lax.psum(reduced[2].astype(jnp.bfloat16), "dp").astype(jnp.float32),
        lax.psum(reduced[3].astype(jnp.bfloat16), "dp").astype(jnp.float32),
        lax.psum(reduced[4].astype(jnp.bfloat16), "dp").astype(jnp.float32),
        lax.psum(reduced[5].astype(jnp.bfloat16), "dp").astype(jnp.float32),
        lax.psum(reduced[6].astype(jnp.bfloat16), "dp").astype(jnp.float32),
        lax.psum(reduced[7].astype(jnp.bfloat16), "dp").astype(jnp.float32),
        lax.psum(reduced[8].astype(jnp.bfloat16), "dp").astype(jnp.float32),
        lax.psum(reduced[9].astype(jnp.bfloat16), "dp").astype(jnp.float32),
        lax.psum(reduced[10].astype(jnp.bfloat16), "dp").astype(jnp.float32),
        lax.psum(reduced[11].astype(jnp.bfloat16), "dp").astype(jnp.float32),
        lax.psum(reduced[12].astype(jnp.bfloat16), "dp").astype(jnp.float32),
        lax.psum(reduced[13].astype(jnp.bfloat16), "dp").astype(jnp.float32),
        lax.psum(reduced[14].astype(jnp.bfloat16), "dp").astype(jnp.float32),
    )
    return (
        output,
        d_tokens,
        summed[0],
        summed[6][0],
        summed[1],
        summed[2],
        summed[7][0],
        summed[3],
        summed[8][0],
        summed[4],
        summed[9][0],
        summed[5],
        summed[10][0],
        summed[11][0],
        summed[12][0],
        summed[13][0],
        summed[14][0],
    )


def solution(mesh):
    in_specs = (
        P(("dp", "row"), "col"),
        P(("dp", "row"), None),
        P(("dp", "row"), "col"),
        P("row", "col"),
        P("col"),
        P("row", "col"),
        P("row", "col"),
        P("col"),
        P("row", "col"),
        P("col"),
        P("row", "col"),
        P("col"),
        P("row", "col"),
        P("col"),
        P("col"),
        P("col"),
        P("col"),
        P("col"),
    )
    out_specs = (
        P(("dp", "row"), "col"),
        P(("dp", "row"), "col"),
        P("row", "col"),
        P("col"),
        P("row", "col"),
        P("row", "col"),
        P("col"),
        P("row", "col"),
        P("col"),
        P("row", "col"),
        P("col"),
        P("row", "col"),
        P("col"),
        P("col"),
        P("col"),
        P("col"),
        P("col"),
    )
    return jax.shard_map(body, mesh=mesh, in_specs=in_specs, out_specs=out_specs, check_vma=False)
```

profile of v0, /device:TPU:0, one launch (start us, length us, event | category | flops | bytes accessed | tf_op | source)
XLA Modules:
  0.0 867.2 jit_solution(18312474108476060332)
XLA Ops:
  14.0 26.2 %all-gather.15.cloned.1.call-done = bf16[1024,512]{1,0:T(8,128)(2,1)} async-done(((bf16[256,512]{1,0:T(8,128)(2,1)}), bf16[1024,512]{1,0:T(8,128)(2,1)}) %all-gather.15.cloned.1.call-update) | async-done | bytes 1048592 | tf_op jit(solution)/shard_map/all_gather | solution.py:165
  40.3 11.6 %all-gather.11.cloned.1.call-done = bf16[1024,1024]{1,0:T(8,128)(2,1)} async-done(((bf16[1024,512]{1,0:T(8,128)(2,1)}), bf16[1024,1024]{1,0:T(8,128)(2,1)}) %all-gather.11.cloned.1.call-update) | async-done | bytes 2097168 | tf_op jit(solution)/shard_map/all_gather | solution.py:30
  55.2 27.5 %all-gather.17.cloned.1.call-done = bf16[1024,512]{1,0:T(8,128)(2,1)} async-done(((bf16[256,512]{1,0:T(8,128)(2,1)}), bf16[1024,512]{1,0:T(8,128)(2,1)}) %all-gather.17.cloned.1.call-update) | async-done | bytes 1048592 | tf_op jit(solution)/shard_map/all_gather | solution.py:166
  98.7 12.8 %all-gather.13.cloned.1.call-done = bf16[1024,512]{1,0:T(8,128)(2,1)} async-done(((bf16[256,512]{1,0:T(8,128)(2,1)}), bf16[1024,512]{1,0:T(8,128)(2,1)}) %all-gather.13.cloned.1.call-update) | async-done | bytes 1048592 | tf_op jit(solution)/shard_map/all_gather | solution.py:167
  140.2 12.2 %all-gather.19.cloned.1.call-done = bf16[1024,1024]{0,1:T(8,128)(2,1)} async-done(((bf16[1024,512]{0,1:T(8,128)(2,1)}), bf16[1024,1024]{0,1:T(8,128)(2,1)}) %all-gather.19.cloned.1.call-update) | async-done | bytes 2097168 | tf_op jit(solution)/shard_map/all_gather | solution.py:30
  171.5 83.5 %all-gather.25.cloned.1.call-done = bf16[1024,2048]{1,0:T(8,128)(2,1)} async-done(((bf16[256,2048]{1,0:T(8,128)(2,1)}), bf16[1024,2048]{1,0:T(8,128)(2,1)}) %all-gather.25.cloned.1.call-update) | async-done | bytes 4194320 | tf_op jit(solution)/shard_map/all_gather | solution.py:169
  255.1 26.6 %multiply_convert_fusion.2 = (bf16[1024,2048]{1,0:T(8,128)(2,1)}, f32[1024,2048]{1,0:T(8,128)}, f32[1024,2048]{1,0:T(8,128)}) fusion(f32[2048]{0:T(1024)S(1)} %convert_element_type.255, bf16[1024,1024]{0,1:T(8,128)(2,1)} %all-gather.23.cloned.1.call-done, bf16[1024,2048]{1,0:T(8,128)(2,1)} %all-gather.25.cloned.1.call-done), kind=kOutput, calls=%fused_computation.23 | convolution fusion | flops 4433379328 | bytes 27271168 | tf_op jit(solution)/shard_map/dot_general | solution.py:14
  283.3 52.7 %all-gather.29.cloned.1.call-done = bf16[4096,512]{1,0:T(8,128)(2,1)} async-done(((bf16[1024,512]{1,0:T(8,128)(2,1)}), bf16[4096,512]{1,0:T(8,128)(2,1)}) %all-gather.29.cloned.1.call-update) | async-done | bytes 4194320 | tf_op jit(solution)/shard_map/all_gather | solution.py:170
  336.0 19.8 %all-gather.27.cloned.1.call-done = bf16[1024,4096]{1,0:T(8,128)(2,1)} async-done(((bf16[1024,2048]{1,0:T(8,128)(2,1)}), bf16[1024,4096]{1,0:T(8,128)(2,1)}) %all-gather.27.cloned.1.call-update) | async-done | bytes 8388624 | tf_op jit(solution)/shard_map/all_gather | solution.py:186
  355.8 10.9 %fusion.49 = (f32[1024]{0:T(1024)S(1)}, f32[1024]{0:T(1024)S(1)}, f32[1024,512]{0,1:T(8,128)}) fusion(f32[512]{0:T(512)S(1)} %convert_element_type.257, bf16[1024,4096]{1,0:T(8,128)(2,1)} %all-gather.27.cloned.1.call-done, bf16[4096,512]{1,0:T(8,128)(2,1)} %all-gather.29.cloned.1.call-done, bf16[1024,512]{0,1:T(8,128)(2,1)} %add_convert_fusion.4), kind=kOutput, calls=%fused_computation.121 | convolution fusion | flops 4298110976 | bytes 15738880 | tf_op jit(solution)/shard_map/dot_general | solution.py:14
  389.3 27.6 %reduce-scatter.11.cloned.1.call-done = f32[1024,2048]{1,0:T(8,128)} async-done(((f32[1024,4096]{1,0:T(8,128)}), f32[1024,2048]{1,0:T(8,128)}) %reduce-scatter.11.cloned.1.call-update) | async-done | bytes 8388624 | tf_op jit(solution)/shard_map/reduce_scatter | solution.py:198
  416.9 10.4 %fusion.53 = (bf16[2048]{0:T(1024)(128)(2,1)S(1)}, bf16[1024,2048]{1,0:T(8,128)(2,1)S(1)}) fusion(f32[1024,2048]{1,0:T(8,128)} %reduce-scatter.11.cloned.1.call-done, f32[1024,2048]{1,0:T(8,128)} %get-tuple-element.121, f32[1024,2048]{1,0:T(8,128)} %get-tuple-element.140, f32[2048]{0:T(1024)S(1)} %convert_element_type.255), kind=kLoop, calls=%fused_computation.124 | loop fusion | flops 33552384 | bytes 29372416 | tf_op jit(solution)/shard_map/reduce_sum | solution.py:140
  435.5 13.4 %reduce-scatter.13.cloned.1.call-done = f32[1024,512]{0,1:T(8,128)} async-done(((f32[1024,1024]{0,1:T(8,128)}), f32[1024,512]{0,1:T(8,128)}) %reduce-scatter.13.cloned.1.call-update) | async-done | bytes 2097168 | tf_op jit(solution)/shard_map/reduce_scatter | solution.py:34
  510.5 13.6 %multiply_reduce_fusion.1 = (f32[8,512]{1,0:T(8,128)S(1)}, f32[8,512,1024]{2,1,0:T(8,128)}) fusion(f32[8,512,1024]{2,1,0:T(8,128)} %copy-done.1, f32[8,512]{1,0:T(8,128)S(1)} %log_add_fusion.1, bf16[512,8,64]{0,2,1:T(8,128)(2,1)S(1)} %bitcast.99, bf16[1024,8,64]{0,2,1:T(8,128)(2,1)} %bitcast.104), kind=kOutput, calls=%fused_computation.4 | convolution fusion | flops 549449728 | bytes 35160064 | tf_op jit(solution)/shard_map/qhd,khd->hqk/dot_general | solution.py:110
  524.1 11.1 %multiply_reduce_fusion = (f32[8,512]{1,0:T(8,128)S(1)}, f32[8,512,1024]{2,1,0:T(8,128)}) fusion(f32[8,512,1024]{2,1,0:T(8,128)} %copy-done, f32[8,512]{1,0:T(8,128)S(1)} %log_add_fusion, bf16[512,8,64]{0,2,1:T(8,128)(2,1)S(1)} %bitcast.97, bf16[1024,8,64]{0,2,1:T(8,128)(2,1)S(1)} %bitcast.105), kind=kOutput, calls=%fused_computation.1 | convolution fusion | flops 549449728 | bytes 35160064 | tf_op jit(solution)/shard_map/qhd,khd->hqk/dot_general | solution.py:110
  535.6 15.8 %multiply_convert_fusion.1 = bf16[8,512,1024]{2,1,0:T(8,128)(2,1)} fusion(f32[8,512,1024]{2,1,0:T(8,128)} %get-tuple-element.145, f32[8,512,1024]{2,1,0:T(8,128)} %copy-done.1, f32[8,512]{1,0:T(8,128)S(1)} %get-tuple-element.144, f32[8,512]{1,0:T(8,128)S(1)} %log_add_fusion.1), kind=kLoop, calls=%fused_computation.3 | loop fusion | flops 16777216 | bytes 41975808 | tf_op jit(solution)/shard_map/convert_element_type | solution.py:114
  587.8 49.1 %reduce-scatter.27.cloned.1.call-done = bf16[256,2048]{1,0:T(8,128)(2,1)} async-done(((bf16[1024,2048]{1,0:T(8,128)(2,1)}), bf16[256,2048]{1,0:T(8,128)(2,1)}) %reduce-scatter.27.cloned.1.call-update) | async-done | bytes 1048592 | tf_op jit(solution)/shard_map/reduce_scatter | solution.py:244
  636.9 30.0 %reduce-scatter.25.cloned.1.call-done = bf16[256,512]{1,0:T(8,128)(2,1)} async-done(((bf16[1024,512]{1,0:T(8,128)(2,1)}), bf16[256,512]{1,0:T(8,128)(2,1)}) %reduce-scatter.25.cloned.1.call-update) | async-done | bytes 262160 | tf_op jit(solution)/shard_map/reduce_scatter | solution.py:241
  666.8 27.9 %reduce-scatter.23.cloned.1.call-done = bf16[256,512]{0,1:T(8,128)(2,1)} async-done(((bf16[1024,512]{0,1:T(8,128)(2,1)}), bf16[256,512]{0,1:T(8,128)(2,1)}) %reduce-scatter.23.cloned.1.call-update) | async-done | bytes 262160 | tf_op jit(solution)/shard_map/reduce_scatter | solution.py:238
  694.8 28.1 %reduce-scatter.21.cloned.1.call-done = bf16[256,512]{0,1:T(8,128)(2,1)} async-done(((bf16[1024,512]{0,1:T(8,128)(2,1)}), bf16[256,512]{0,1:T(8,128)(2,1)}) %reduce-scatter.21.cloned.1.call-update) | async-done | bytes 262160 | tf_op jit(solution)/shard_map/reduce_scatter | solution.py:235
  722.8 28.1 %reduce-scatter.19.cloned.1.call-done = bf16[256,512]{0,1:T(8,128)(2,1)} async-done(((bf16[1024,512]{0,1:T(8,128)(2,1)}), bf16[256,512]{0,1:T(8,128)(2,1)}) %reduce-scatter.19.cloned.1.call-update) | async-done | bytes 262160 | tf_op jit(solution)/shard_map/reduce_scatter | solution.py:232
  763.8 17.1 %all-reduce.13 = (bf16[4,512]{1,0:T(4,128)(2,1)S(1)}, bf16[4,512]{1,0:T(4,128)(2,1)S(1)}, bf16[4,512]{1,0:T(4,128)(2,1)S(1)}, bf16[4,2048]{1,0:T(4,128)(2,1)S(1)...) all-reduce(bf16[4,512]{1,0:T(4,128)(2,1)S(1)} %broadcast_in_dim.47,, ...), channel_id=7, replica_groups=mesh['dp'=4,'row'=4,'col'=2] {'row'}, use_global_device_ids=true, to_apply=%region_29.30.clone | all-reduce | flops 24576 | bytes 98304
  787.0 16.2 %all-reduce.14 = (bf16[512]{0:T(512)(128)(2,1)S(1)}, bf16[512]{0:T(512)(128)(2,1)S(1)}, bf16[512]{0:T(512)(128)(2,1)S(1)}, bf16[2048]{0:T(1024)(128)(2,1)S(1)}, ...) all-reduce(bf16[512]{0:T(512)(128)(2,1)S(1)} %fusion.38, ...), channel_id=1, replica_groups=mesh['dp'=4,'row'=4,'col'=2] {'dp'}, use_global_device_ids=true, to_apply=%region_30.31 | all-reduce | flops 6144 | bytes 24576 | tf_op jit(solution)/shard_map/psum | solution.py:285
  808.4 33.8 %all-reduce.18.cloned.1.call-done = (bf16[256,512]{0,1:T(8,128)(2,1)}, bf16[256,512]{0,1:T(8,128)(2,1)}, bf16[256,512]{0,1:T(8,128)(2,1)}, bf16[256,512]{1,0:T(8...) async-done(((bf16[256,512]{0,1:T(8,128)(2,1)}, bf16[256,512]{0,1:T(8,128)(2,1)}, bf16[256,512]{0,1:T(8,128)(2,1)}, bf16[256,512]{1,0:T(8,128)(2,1)}, ...) | async-done | bytes 3145744 | tf_op jit(solution)/shard_map/psum | solution.py:279
  (245 shorter events, 245.4 us)
Async XLA Ops:
  7.2 33.1 %all-gather.15.cloned.1.call-start = ((), (), s32[]{:S(2)}) async-start(), calls=%async_computation.12 | async-start | bytes 1310720 | tf_op jit(solution)/shard_map/all_gather | solution.py:165
  7.9 44.0 %all-gather.11.cloned.1.call-start = ((), (), s32[]{:S(2)}) async-start(), calls=%async_computation.10 | async-start | bytes 3145728 | tf_op jit(solution)/shard_map/all_gather | solution.py:30
  8.7 73.9 %all-gather.17.cloned.1.call-start = ((), (), s32[]{:S(2)}) async-start(), calls=%async_computation.13 | async-start | bytes 1310720 | tf_op jit(solution)/shard_map/all_gather | solution.py:166
  9.4 102.1 %all-gather.13.cloned.1.call-start = ((), (), s32[]{:S(2)}) async-start(), calls=%async_computation.11 | async-start | bytes 1310720 | tf_op jit(solution)/shard_map/all_gather | solution.py:167
  10.0 130.3 %all-gather.21.cloned.1.call-start = ((), (), s32[]{:S(2)}) async-start(), calls=%async_computation.15 | async-start | bytes 1310720 | tf_op jit(solution)/shard_map/all_gather | solution.py:168
  10.6 141.9 %all-gather.19.cloned.1.call-start = ((), (), s32[]{:S(2)}) async-start(), calls=%async_computation.14 | async-start | bytes 3145728 | tf_op jit(solution)/shard_map/all_gather | solution.py:30
  136.7 34.8 %all-gather.23.cloned.1.call-start = ((), (), s32[]{:S(2)}) async-start(), calls=%async_computation.16 | async-start | bytes 3145728 | tf_op jit(solution)/shard_map/all_gather | solution.py:30
  155.8 293.1 %copy-start.4 = (f32[1024,512]{0,1:T(8,128)}, f32[1024,512]{0,1:T(8,128)S(1)}, u32[]{:S(2)}) copy-start(f32[1024,512]{0,1:T(8,128)S(1)} %get-tuple-element.139) | copy-start | bytes 6291460
  159.6 95.4 %all-gather.25.cloned.1.call-start = ((), (), s32[]{:S(2)}) async-start(), calls=%async_computation.17 | async-start | bytes 5242880 | tf_op jit(solution)/shard_map/all_gather | solution.py:169
  160.4 175.6 %all-gather.29.cloned.1.call-start = ((), (), s32[]{:S(2)}) async-start(), calls=%async_computation.19 | async-start | bytes 5242880 | tf_op jit(solution)/shard_map/all_gather | solution.py:170
  161.1 194.7 %all-gather.27.cloned.1.call-start = ((), (), s32[]{:S(2)}) async-start(), calls=%async_computation.18 | async-start | bytes 12582912 | tf_op jit(solution)/shard_map/all_gather | solution.py:186
  161.2 120.6 %copy-start.33 = (bf16[512]{0:T(512)(128)(2,1)S(1)}, bf16[512]{0:T(512)(128)(2,1)}, u32[]{:S(2)}) copy-start(bf16[512]{0:T(512)(128)(2,1)} %param.34) | copy-start | bytes 3076
  161.2 120.6 %copy-start.34 = (bf16[512]{0:T(512)(128)(2,1)S(1)}, bf16[512]{0:T(512)(128)(2,1)}, u32[]{:S(2)}) copy-start(bf16[512]{0:T(512)(128)(2,1)} %param.31) | copy-start | bytes 3076
  281.7 135.2 %reduce-scatter.11.cloned.1.call-start = ((), (), s32[]{:S(2)}) async-start(), calls=%async_computation.20 | async-start | bytes 25165824 | tf_op jit(solution)/shard_map/reduce_scatter | solution.py:198
  389.3 59.6 %reduce-scatter.13.cloned.1.call-start = ((), (), s32[]{:S(2)}) async-start(), calls=%async_computation.21 | async-start | bytes 6291456 | tf_op jit(solution)/shard_map/reduce_scatter | solution.py:34
  435.4 52.6 %reduce-scatter.15.cloned.1.call-start = ((), (), s32[]{:S(2)}) async-start(), calls=%async_computation.22 | async-start | bytes 6291456 | tf_op jit(solution)/shard_map/reduce_scatter | solution.py:34
  463.6 124.2 %reduce-scatter.29.cloned.1.call-start = ((), (), s32[]{:S(2)}) async-start(), calls=%async_computation.29 | async-start | bytes 5242880 | tf_op jit(solution)/shard_map/reduce_scatter | solution.py:247
  473.6 163.2 %reduce-scatter.27.cloned.1.call-start = ((), (), s32[]{:S(2)}) async-start(), calls=%async_computation.28 | async-start | bytes 5242880 | tf_op jit(solution)/shard_map/reduce_scatter | solution.py:244
  483.7 183.1 %reduce-scatter.25.cloned.1.call-start = ((), (), s32[]{:S(2)}) async-start(), calls=%async_computation.27 | async-start | bytes 1310720 | tf_op jit(solution)/shard_map/reduce_scatter | solution.py:241
  487.8 207.0 %reduce-scatter.23.cloned.1.call-start = ((), (), s32[]{:S(2)}) async-start(), calls=%async_computation.26 | async-start | bytes 1310720 | tf_op jit(solution)/shard_map/reduce_scatter | solution.py:238
  535.3 187.6 %reduce-scatter.21.cloned.1.call-start = ((), (), s32[]{:S(2)}) async-start(), calls=%async_computation.25 | async-start | bytes 1310720 | tf_op jit(solution)/shard_map/reduce_scatter | solution.py:235
  575.3 175.7 %reduce-scatter.19.cloned.1.call-start = ((), (), s32[]{:S(2)}) async-start(), calls=%async_computation.24 | async-start | bytes 1310720 | tf_op jit(solution)/shard_map/reduce_scatter | solution.py:232
  587.7 254.5 %all-reduce.18.cloned.1.call-start = ((), (), s32[]{:S(2)}) async-start(), calls=%async_computation.30 | async-start | bytes 6291456 | tf_op jit(solution)/shard_map/psum | solution.py:279
  751.0 105.6 %reduce-scatter.17.cloned.1.call-start = ((), (), s32[]{:S(2)}) async-start(), calls=%async_computation.23 | async-start | bytes 6291456 | tf_op jit(solution)/shard_map/reduce_scatter | solution.py:34
  (43 other events, 478.3 us)
Sparse Core Ops, SparseCore 0:
  9.6 30.6 all-gather.14
  41.8 10.0 all-gather.10
  53.5 29.0 all-gather.16
  84.0 27.4 all-gather.12
  112.9 27.2 all-gather.20
  142.2 10.1 all-gather.18
  159.8 11.7 all-gather.22
  173.1 81.9 all-gather.24
  256.6 79.2 all-gather.28
  337.4 18.3 all-gather.26
  389.4 27.4 reduce-scatter.10
  435.6 13.2 reduce-scatter.12
  463.7 13.3 reduce-scatter.14
  479.3 78.0 reduce-scatter.28
  559.6 77.2 reduce-scatter.26
  639.1 27.6 reduce-scatter.24
  668.9 25.7 reduce-scatter.22
  697.0 25.7 reduce-scatter.20
  725.1 25.7 reduce-scatter.18
  755.0 87.2 all-reduce.17
  844.5 12.0 reduce-scatter.16
where the time goes:
time: 873 us; the launch traced here: 867 us
  waiting for transfers between devices  503 us (58%)
  matrix products  186 us (21%)
  other arithmetic  79.1 us (9%)
  blocking collectives  43.6 us (5%)
  local copies, waits for them, and re-layouts  38.1 us (4%)
  between operations  15.7 us (2%)
    all_gather x1, waiting for transfers between devices, body(): lax.all_gather(w_up, 'row', axis=0, tiled=True)  83.5 us
    all_gather x1, waiting for transfers between devices, body(): lax.all_gather(w_down, 'row', axis=0, tiled=True)  52.7 us
    dot_general x6, matrix products, matmul(): return jnp.dot(left, right, preferred_element_type=jnp.float32)  50.2 us
    reduce_scatter x1, waiting for transfers between devices, body(): lax.psum_scatter(d_w_up.astype(jnp.bfloat16), 'row', scatter_dimension=0,...  49.1 us
    all_gather x3, waiting for transfers between devices, whole_rows(): return lax.all_gather(part, 'col', axis=1, tiled=True)  34.2 us
    psum x1, waiting for transfers between devices, body(): lax.psum(reduced[0].astype(jnp.bfloat16), 'dp').astype(jnp.float32)  33.8 us
    dot_general x6, matrix products, matmul_tn(): lax.dot_general(left, right, (((0,), (0,)), ((), ())), preferred_element_...  30.4 us
    reduce_scatter x1, waiting for transfers between devices, body(): lax.psum_scatter(d_w_out.astype(jnp.bfloat16), 'row', scatter_dimension=0...  30 us
  transfers between devices with their start and end apart: 21, of which 19 were waited for; matrix products, arithmetic and copies ran while one was open for 26% of the time, Pallas kernels for 0%

commit v1 on v0

v1 whole, which is shorter than its diff:
```python
import jax
import jax.numpy as jnp
from jax import lax
from jax.sharding import PartitionSpec as P

HEAD_DIM = 64


EPSILON = 1e-05
SCALE = 0.125


def matmul(left, right):
    return jnp.dot(left, right, preferred_element_type=jnp.float32)


def matmul_tn(left, right):
    return lax.dot_general(
        left, right, (((0,), (0,)), ((), ())), preferred_element_type=jnp.float32
    )


def matmul_nt(left, right):
    return lax.dot_general(
        left, right, (((1,), (1,)), ((), ())), preferred_element_type=jnp.float32
    )


def masked_scores(query_block, key_three, segment_ids, begin, block):
    raw = (
        jnp.einsum("qhd,khd->hqk", query_block, key_three, preferred_element_type=jnp.float32)
        * SCALE
    )
    same = segment_ids[begin : begin + block, None] == segment_ids[None, :]
    return jnp.where(same[None], raw, -1e30)


def attend(queries, key_rows, value_rows, segment_ids):
    count = queries.shape[0]
    heads_here = queries.shape[1] // HEAD_DIM
    block = min(512, count)
    query_three = queries.reshape(count, heads_here, HEAD_DIM)
    key_three = key_rows.reshape(count, heads_here, HEAD_DIM)
    value_three = value_rows.reshape(count, heads_here, HEAD_DIM)
    pieces = []
    totals = []
    for begin in range(0, count, block):
        scores = masked_scores(
            query_three[begin : begin + block], key_three, segment_ids, begin, block
        )
        row_top = jnp.max(scores, axis=2, keepdims=True)
        expo = jnp.exp(scores - row_top)
        total = jnp.sum(expo, axis=2, keepdims=True)
        probs = (expo / total).astype(jnp.bfloat16)
        pieces.append(
            jnp.einsum("hqk,khd->qhd", probs, value_three, preferred_element_type=jnp.float32)
        )
        totals.append((row_top + jnp.log(total))[:, :, 0])
    context = (
        jnp.concatenate(pieces, axis=0).reshape(count, heads_here * HEAD_DIM).astype(jnp.bfloat16)
    )
    return (context, jnp.concatenate(totals, axis=1))


def attend_back(queries, key_rows, value_rows, segment_ids, log_total, d_context):
    count = queries.shape[0]
    heads_here = queries.shape[1] // HEAD_DIM
    block = min(512, count)
    query_three = queries.reshape(count, heads_here, HEAD_DIM)
    key_three = key_rows.reshape(count, heads_here, HEAD_DIM)
    value_three = value_rows.reshape(count, heads_here, HEAD_DIM)
    grad_three = d_context.reshape(count, heads_here, HEAD_DIM)
    d_keys = jnp.zeros((count, heads_here, HEAD_DIM), jnp.float32)
    d_values = jnp.zeros((count, heads_here, HEAD_DIM), jnp.float32)
    pieces = []
    for begin in range(0, count, block):
        query_block = query_three[begin : begin + block]
        grad_block = grad_three[begin : begin + block]
        scores = masked_scores(query_block, key_three, segment_ids, begin, block)
        probs = jnp.exp(scores - log_total[:, begin : begin + block, None])
        d_probs = jnp.einsum(
            "qhd,khd->hqk", grad_block, value_three, preferred_element_type=jnp.float32
        )
        inner = jnp.sum(probs * d_probs, axis=2, keepdims=True)
        d_scores = (probs * (d_probs - inner)).astype(jnp.bfloat16)
        pieces.append(
            jnp.einsum("hqk,khd->qhd", d_scores, key_three, preferred_element_type=jnp.float32)
            * SCALE
        )
        d_keys = (
            d_keys
            + jnp.einsum("hqk,qhd->khd", d_scores, query_block, preferred_element_type=jnp.float32)
            * SCALE
        )
        d_values = d_values + jnp.einsum(
            "hqk,qhd->khd",
            probs.astype(jnp.bfloat16),
            grad_block,
            preferred_element_type=jnp.float32,
        )
    width = heads_here * HEAD_DIM
    d_queries = jnp.concatenate(pieces, axis=0).reshape(count, width).astype(jnp.bfloat16)
    return (
        d_queries,
        d_keys.reshape(count, width).astype(jnp.bfloat16),
        d_values.reshape(count, width).astype(jnp.bfloat16),
    )


def column_sum(values):
    return jnp.sum(values.astype(jnp.float32), axis=0)


def swapped(part):
    return lax.ppermute(part, "col", [(0, 1), (1, 0)])


def ordered(own, other, core, axis):
    return jnp.where(
        core == 0,
        jnp.concatenate([own, other], axis=axis),
        jnp.concatenate([other, own], axis=axis),
    )


def whole_features(part, core):
    return ordered(part, swapped(part), core, part.ndim - 1)


def half_of(values, index, axis):
    size = values.shape[axis] // 2
    return lax.dynamic_slice_in_dim(values, index * size, size, axis)


def whole_weight(block):
    rows = block.shape[0] // lax.axis_size("dp")
    part = lax.dynamic_slice_in_dim(block, lax.axis_index("dp") * rows, rows, 0)
    return lax.all_gather(part, ("row", "dp"), axis=0, tiled=True)


def reduced_weight(grad):
    part = lax.psum_scatter(grad, ("row", "dp"), scatter_dimension=0, tiled=True)
    return lax.all_gather(part, "dp", axis=0, tiled=True).astype(jnp.float32)


def norm_forward(resid, gain, shift):
    center = jnp.mean(resid, axis=1, keepdims=True)
    inverse = lax.rsqrt(
        jnp.mean(resid * resid, axis=1, keepdims=True) - center * center + EPSILON
    )
    normed = (resid - center) * inverse
    return (normed * gain + shift, normed, inverse)


def norm_backward(grad, normed, inverse, gain):
    scaled = grad * gain
    first = jnp.mean(scaled, axis=1, keepdims=True)
    second = jnp.mean(scaled * normed, axis=1, keepdims=True)
    return inverse * (scaled - first - normed * second)


def body(
    tokens,
    segment,
    cotangent,
    w_query,
    b_query,
    w_key,
    w_value,
    b_value,
    w_out,
    b_out,
    w_up,
    b_up,
    w_down,
    b_down,
    gain_one,
    shift_one,
    gain_two,
    shift_two,
):
    core = lax.axis_index("col")
    half = w_query.shape[1]
    w_qkv = whole_weight(jnp.concatenate([w_query, w_key, w_value], axis=1))
    wo_half = whole_weight(w_out)
    wu = whole_weight(w_up)
    wd_half = whole_weight(w_down)
    token_rows = whole_features(tokens, core)
    cotangent_rows = whole_features(cotangent, core)
    vectors = whole_features(
        jnp.stack([b_out, b_down, gain_one, shift_one, gain_two, shift_two]), core
    ).astype(jnp.float32)
    bias_out, bias_down, gain1, shift1, gain2, shift2 = [vectors[i] for i in range(6)]
    wo = whole_features(wo_half, core)
    wd = ordered(
        half_of(wd_half, core, 0), swapped(half_of(wd_half, 1 - core, 0)), core, 1
    )
    segment_ids = segment[0]

    b_qkv = jnp.concatenate([b_query, jnp.zeros_like(b_query), b_value]).astype(jnp.float32)
    qkv = (matmul(token_rows, w_qkv) + b_qkv).astype(jnp.bfloat16)
    queries, key_rows, value_rows = (qkv[:, i * half : (i + 1) * half] for i in range(3))
    context, log_total = attend(queries, key_rows, value_rows, segment_ids)
    context_rows = whole_features(context, core)
    first_sum = token_rows.astype(jnp.float32) + (matmul(context_rows, wo) + bias_out)
    hidden_f, normed_one, inverse_one = norm_forward(first_sum, gain1, shift1)
    hidden = hidden_f.astype(jnp.bfloat16)
    pre_act = matmul(hidden, wu) + b_up.astype(jnp.float32)
    cdf = 0.5 * (1.0 + lax.erf(pre_act * (0.5**0.5)))
    activated = (pre_act * cdf).astype(jnp.bfloat16)
    slope = cdf + pre_act * (jnp.exp(-0.5 * pre_act * pre_act) * 0.3989422804014327)
    part = matmul(activated, wd).astype(jnp.bfloat16)
    ffn_out = part.astype(jnp.float32) + swapped(part).astype(jnp.float32) + bias_down
    second_sum = hidden.astype(jnp.float32) + ffn_out
    final, normed_two, inverse_two = norm_forward(second_sum, gain2, shift2)
    output = half_of(final.astype(jnp.bfloat16), core, 1)
    y = cotangent_rows.astype(jnp.float32)
    second_grad = norm_backward(y, normed_two, inverse_two, gain2)
    d_gain_two = jnp.sum(y * normed_two, axis=0)
    d_shift_two = jnp.sum(y, axis=0)
    ffn_grad = second_grad.astype(jnp.bfloat16)
    d_w_down = matmul_tn(activated, ffn_grad).astype(jnp.bfloat16)
    d_w_down = ordered(
        half_of(d_w_down, core, 1), swapped(half_of(d_w_down, 1 - core, 1)), core, 0
    )
    o_w_down = reduced_weight(d_w_down)
    d_b_down = column_sum(ffn_grad)
    pre_grad = (matmul_nt(ffn_grad, wd) * slope).astype(jnp.bfloat16)
    d_w_up = matmul_tn(hidden, pre_grad).astype(jnp.bfloat16)
    o_w_up = reduced_weight(d_w_up)
    d_b_up = column_sum(pre_grad)
    hidden_part = matmul_nt(pre_grad, wu).astype(jnp.bfloat16)
    hidden_grad = second_grad + (
        hidden_part.astype(jnp.float32) + swapped(hidden_part).astype(jnp.float32)
    )
    first_grad = norm_backward(hidden_grad, normed_one, inverse_one, gain1)
    d_gain_one = jnp.sum(hidden_grad * normed_one, axis=0)
    d_shift_one = jnp.sum(hidden_grad, axis=0)
    branch_grad = first_grad.astype(jnp.bfloat16)
    branch_half = half_of(branch_grad, core, 1)
    d_w_out = matmul_tn(context_rows, branch_half).astype(jnp.bfloat16)
    o_w_out = reduced_weight(d_w_out)
    d_b_out = column_sum(branch_grad)
    context_grad = matmul_nt(branch_grad, half_of(wo, core, 0)).astype(jnp.bfloat16)
    query_grad, key_grad, value_grad = attend_back(
        queries, key_rows, value_rows, segment_ids, log_total, context_grad
    )
    qkv_grad = jnp.concatenate([query_grad, key_grad, value_grad], axis=1)
    d_w_qkv = matmul_tn(token_rows, qkv_grad).astype(jnp.bfloat16)
    o_w_qkv = reduced_weight(d_w_qkv)
    d_b_qkv = column_sum(qkv_grad)
    token_part = matmul_nt(qkv_grad, w_qkv).astype(jnp.bfloat16)
    token_sum = half_of(token_part, core, 1).astype(jnp.float32) + swapped(
        half_of(token_part, 1 - core, 1)
    ).astype(jnp.float32)
    d_tokens = (token_sum + half_of(first_grad, core, 1)).astype(jnp.bfloat16)

    wide = half_of(
        jnp.stack([d_b_out, d_b_down, d_gain_one, d_shift_one, d_gain_two, d_shift_two]), core, 1
    )
    sums = lax.psum(
        jnp.concatenate([wide.reshape(-1), d_b_qkv, d_b_up]).reshape(-1, 128), ("row", "dp")
    ).reshape(-1)
    pieces = [sums[i * half : (i + 1) * half] for i in range(9)]
    return (
        output,
        d_tokens,
        o_w_qkv[:, :half],
        pieces[6],
        o_w_qkv[:, half : 2 * half],
        o_w_qkv[:, 2 * half :],
        pieces[8],
        o_w_out,
        pieces[0],
        o_w_up,
        sums[9 * half :],
        o_w_down,
        pieces[1],
        pieces[2],
        pieces[3],
        pieces[4],
        pieces[5],
    )


def solution(mesh):
    in_specs = (
        P(("dp", "row"), "col"),
        P(("dp", "row"), None),
        P(("dp", "row"), "col"),
        P("row", "col"),
        P("col"),
        P("row", "col"),
        P("row", "col"),
        P("col"),
        P("row", "col"),
        P("col"),
        P("row", "col"),
        P("col"),
        P("row", "col"),
        P("col"),
        P("col"),
        P("col"),
        P("col"),
        P("col"),
    )
    out_specs = (
        P(("dp", "row"), "col"),
        P(("dp", "row"), "col"),
        P("row", "col"),
        P("col"),
        P("row", "col"),
        P("row", "col"),
        P("col"),
        P("row", "col"),
        P("col"),
        P("row", "col"),
        P("col"),
        P("row", "col"),
        P("col"),
        P("col"),
        P("col"),
        P("col"),
        P("col"),
    )
    return jax.shard_map(body, mesh=mesh, in_specs=in_specs, out_specs=out_specs, check_vma=False)
```

time: 873 us -> 836 us (0.958)
  waiting for transfers between devices: 503 us -> 420 us
  blocking collectives: 43.6 us -> 98.1 us
  matrix products: 186 us -> 168 us
    psum x5 -> x1, blocking collectives: 26.5 us -> 75.2 us  [body(): lax.psum(jnp.concatenate([wide.reshape(-1), d_b_qkv, d_b_up]).reshape(-1,...]
    reduce_scatter x10 -> x4, waiting for transfers between devices: 205 us -> 167 us  [reduced_weight(): lax.psum_scatter(grad, ('row', 'dp'), scatter_dimension=0, tiled=True)]
    psum x1 -> x0, waiting for transfers between devices: 33.8 us -> none  [body(): lax.psum(reduced[0].astype(jnp.bfloat16), 'dp').astype(jnp.float32)]
    all_gather x0 -> x2, blocking collectives: none -> 22.9 us  [reduced_weight(): return lax.all_gather(part, 'dp', axis=0, tiled=True).astype(jnp.float32)]
    unnamed x1 -> x0, blocking collectives: 17.1 us -> none
    dot_general x6 -> x4, matrix products: 50.2 us -> 36.1 us  [matmul(): return jnp.dot(left, right, preferred_element_type=jnp.float32)]
    all_gather x10 -> x6, waiting for transfers between devices: 260 us -> 247 us  [the longest x4 209 us: whole_weight(): return lax.all_gather(part, ('row', 'dp'), axis=0, tiled=True)]
    dynamic_slice x0 -> x9, local copies, waits for them, and re-layouts: none -> 10.2 us  [the longest x6 6.24 us: half_of(): return lax.dynamic_slice_in_dim(values, index * size, size, axis)]
  transfers between devices with their start and end apart: 21 -> 20, of which waited for: 19 -> 10; matrix products, arithmetic and copies ran while one was open for 26% -> 28% of each run, Pallas kernels for 0% -> 0%
where the time goes in v1:
time: 836 us; the launch traced here: 827 us
  waiting for transfers between devices  420 us (50%)
  matrix products  168 us (20%)
  blocking collectives  98.1 us (12%)
  other arithmetic  79.9 us (10%)
  local copies, waits for them, and re-layouts  43 us (5%)
  between operations  15.3 us (2%)
    all_gather x4, waiting for transfers between devices, whole_weight(): return lax.all_gather(part, ('row', 'dp'), axis=0, tiled=True)  209 us
    reduce_scatter x4, waiting for transfers between devices, reduced_weight(): lax.psum_scatter(grad, ('row', 'dp'), scatter_dimension=0, tiled=True)  167 us
    psum x1, blocking collectives, body(): lax.psum(jnp.concatenate([wide.reshape(-1), d_b_qkv, d_b_up]).reshape(-1,...  75.2 us
    all_gather x2, waiting for transfers between devices, reduced_weight(): return lax.all_gather(part, 'dp', axis=0, tiled=True).astype(jnp.float32)  37.7 us
    dot_general x4, matrix products, matmul(): return jnp.dot(left, right, preferred_element_type=jnp.float32)  36.1 us
    dot_general x4, matrix products, matmul_nt(): lax.dot_general(left, right, (((1,), (1,)), ((), ())), preferred_element_...  27.4 us
    dot_general x4, matrix products, matmul_tn(): lax.dot_general(left, right, (((0,), (0,)), ((), ())), preferred_element_...  26.5 us
    all_gather x2, blocking collectives, reduced_weight(): return lax.all_gather(part, 'dp', axis=0, tiled=True).astype(jnp.float32)  22.9 us
  transfers between devices with their start and end apart: 20, of which 10 were waited for; matrix products, arithmetic and copies ran while one was open for 28% of the time, Pallas kernels for 0%

profile of v1, /device:TPU:0, one launch (start us, length us, event | category | flops | bytes accessed | tf_op | source)
XLA Modules:
  0.0 826.6 jit_solution(1632338988681696506)
XLA Ops:
  15.9 53.5 %all-gather.9.cloned.1.call-done = bf16[1024,512]{1,0:T(8,128)(2,1)} async-done(((bf16[64,512]{1,0:T(8,128)(2,1)}), bf16[1024,512]{1,0:T(8,128)(2,1)}) %all-gather.9.cloned.1.call-update) | async-done | bytes 1048592 | tf_op jit(solution)/shard_map/all_gather | solution.py:138
  71.7 68.1 %all-gather.7.cloned.1.call-done = bf16[1024,1536]{1,0:T(8,128)(2,1)} async-done(((bf16[64,1536]{1,0:T(8,128)(2,1)}), bf16[1024,1536]{1,0:T(8,128)(2,1)}) %all-gather.7.cloned.1.call-update) | async-done | bytes 3145744 | tf_op jit(solution)/shard_map/all_gather | solution.py:138
  169.7 7.9 fusion
  177.7 7.9 fusion.36
  194.5 23.2 %all-gather.13.cloned.1.call-done = bf16[4096,512]{1,0:T(8,128)(2,1)} async-done(((bf16[256,512]{1,0:T(8,128)(2,1)}), bf16[4096,512]{1,0:T(8,128)(2,1)}) %all-gather.13.cloned.1.call-update) | async-done | bytes 4194320 | tf_op jit(solution)/shard_map/all_gather | solution.py:138
  222.3 8.5 %fusion.50 = (f32[1024]{0:T(1024)S(1)}, f32[1024]{0:T(1024)S(1)}, f32[1024,1024]{0,1:T(8,128)}) fusion(f32[1024]{0:T(1024)S(1)} %bitcast.148, bf16[1024,512]{0,1:T(8,128)(2,1)} %collective-permute-done.1, bf16[1024,512]{0,1:T(8,128)(2,1)S(1)} %bitcast.120, pred[]{:T(512)S(6)} %eq.24, bf16[1024,512]{0,1:T(8,128)(2,1)} %collective-permute-done.2, ...), kind=kOutput, calls=%fused_computation.140 | convolution fusion | flops 2182084608 | bytes 10498049 | tf_op jit(solution)/shard_map/dot_general | solution.py:14
  230.8 64.3 %all-gather.11.cloned.1.call-done = bf16[1024,2048]{1,0:T(8,128)(2,1)} async-done(((bf16[64,2048]{1,0:T(8,128)(2,1)}), bf16[1024,2048]{1,0:T(8,128)(2,1)}) %all-gather.11.cloned.1.call-update) | async-done | bytes 4194320 | tf_op jit(solution)/shard_map/all_gather | solution.py:138
  295.1 11.6 %multiply_convert_fusion.2 = (bf16[1024,2048]{1,0:T(8,128)(2,1)S(1)}, f32[1024,2048]{1,0:T(8,128)}) fusion(f32[2048]{0:T(1024)S(1)} %convert_element_type.165, bf16[1024,2048]{1,0:T(8,128)(2,1)} %all-gather.11.cloned.1.call-done, f32[1024,1024]{0,1:T(8,128)} %get-tuple-element.126, f32[1024]{0:T(1024)S(1)} %bitcast.132, f32[1024]{0:T(1024)S(1)} %bitcast.122, ...), kind=kOutput, calls=%fused_computation.28 | convolution fusion | flops 4312793088 | bytes 20996096 | tf_op jit(solution)/shard_map/dot_general | solution.py:14
  306.7 9.9 %convolution_convert_fusion.5 = bf16[1024,1024]{0,1:T(8,128)(2,1)} fusion(bf16[1024,2048]{1,0:T(8,128)(2,1)S(1)} %get-tuple-element.127, bf16[2048,512]{1,0:T(8,128)(2,1)} %collective-permute-done.4, bf16[2048,512]{1,0:T(8,128)(2,1)S(1)} %copy-done.21, pred[]{:T(512)S(6)} %eq.24), kind=kOutput, calls=%fused_computation.76 | convolution fusion | flops 4314890240 | bytes 10485761 | tf_op jit(solution)/shard_map/dot_general | solution.py:14
  337.2 11.0 %convert_reduce_fusion = (f32[2048]{0:T(1024)S(1)}, bf16[1024,2048]{1,0:T(8,128)(2,1)}) fusion(f32[1024,2048]{1,0:T(8,128)S(1)} %bitcast.150, f32[2048]{0:T(1024)S(1)} %convert_element_type.165, bf16[1024,1024]{0,1:T(8,128)(2,1)S(1)} %get-tuple-element.81, bf16[2048,512]{1,0:T(8,128)(2,1)} %collective-permute-done.4, bf16[2048,512]{1,0:T(8,128)(2,1)S(1)} %copy-done.22, ...), kind=kOutput, calls=%fused_computation.25 | convolution fusion | flops 4341102592 | bytes 18890752 | tf_op jit(solution)/shard_map/dot_general | solution.py:24
  348.2 8.8 %convolution_convert_fusion.2 = bf16[1024,2048]{1,0:T(8,128)(2,1)} fusion(bf16[1024,2048]{1,0:T(8,128)(2,1)} %get-tuple-element.134, f32[1024,1024]{0,1:T(8,128)S(1)} %copy-done.4, f32[1024]{0:T(1024)S(1)} %bitcast.135, f32[1024]{0:T(1024)S(1)} %bitcast.125, f32[1024]{0:T(1024)S(1)} %get-tuple-element.117, f32[1024]{0:T(1024)S(1)} %get-tuple-element.116), kind=kOutput, calls=%fused_computation.61 | convolution fusion | flops 4302307328 | bytes 12599296 | tf_op jit(solution)/shard_map/dot_general | solution.py:18
  357.1 9.3 %convolution_convert_fusion.4 = bf16[1024,1024]{0,1:T(8,128)(2,1)} fusion(bf16[1024,2048]{1,0:T(8,128)(2,1)} %get-tuple-element.134, bf16[1024,2048]{1,0:T(8,128)(2,1)} %all-gather.11.cloned.1.call-done), kind=kOutput, calls=%fused_computation.75 | convolution fusion | flops 4296015872 | bytes 10485760 | tf_op jit(solution)/shard_map/dot_general | solution.py:24
  396.1 11.8 %multiply_reduce_fusion.1 = (f32[8,512]{1,0:T(8,128)S(1)}, f32[8,512,1024]{2,1,0:T(8,128)}) fusion(f32[8,512,1024]{2,1,0:T(8,128)} %get-tuple-element.125, f32[8,512]{1,0:T(8,128)S(1)} %log_add_fusion.1, bf16[512,8,64]{0,2,1:T(8,128)(2,1)S(1)} %bitcast.109, bf16[1024,8,64]{0,2,1:T(8,128)(2,1)S(1)} %bitcast.100), kind=kOutput, calls=%fused_computation.4 | convolution fusion | flops 549449728 | bytes 35160064 | tf_op jit(solution)/shard_map/qhd,khd->hqk/dot_general | solution.py:81
  411.8 12.4 %multiply_convert_fusion.1 = bf16[8,512,1024]{2,1,0:T(8,128)(2,1)S(1)} fusion(f32[8,512,1024]{2,1,0:T(8,128)} %get-tuple-element.130, f32[8,512,1024]{2,1,0:T(8,128)} %get-tuple-element.125, f32[8,512]{1,0:T(8,128)S(1)} %get-tuple-element.129, f32[8,512]{1,0:T(8,128)S(1)} %log_add_fusion.1), kind=kLoop, calls=%fused_computation.3 | loop fusion | flops 16777216 | bytes 41975808 | tf_op jit(solution)/shard_map/convert_element_type | solution.py:85
  438.2 8.9 %multiply_reduce_fusion = (f32[8,512]{1,0:T(8,128)S(1)}, f32[8,512,1024]{2,1,0:T(8,128)}) fusion(f32[8,512,1024]{2,1,0:T(8,128)S(1)} %bitcast.93, f32[8,512]{1,0:T(8,128)S(1)} %log_add_fusion, bf16[512,8,64]{0,2,1:T(8,128)(2,1)} %bitcast.111, bf16[1024,8,64]{0,2,1:T(8,128)(2,1)S(1)} %bitcast.101), kind=kOutput, calls=%fused_computation.1 | convolution fusion | flops 549449728 | bytes 35160064 | tf_op jit(solution)/shard_map/qhd,khd->hqk/dot_general | solution.py:81
  447.2 10.2 %multiply_convert_fusion = bf16[8,512,1024]{2,1,0:T(8,128)(2,1)} fusion(f32[8,512,1024]{2,1,0:T(8,128)} %get-tuple-element.132, f32[8,512,1024]{2,1,0:T(8,128)S(1)} %bitcast.93, f32[8,512]{1,0:T(8,128)S(1)} %get-tuple-element.131, f32[8,512]{1,0:T(8,128)S(1)} %log_add_fusion), kind=kLoop, calls=%fused_computation | loop fusion | flops 16777216 | bytes 41975808 | tf_op jit(solution)/shard_map/convert_element_type | solution.py:85
  475.9 7.8 add_convert_fusion.3
  503.2 44.6 %reduce-scatter.11.cloned.1.call-done = bf16[256,512]{1,0:T(8,128)(2,1)} async-done(((bf16[4096,512]{1,0:T(8,128)(2,1)}), bf16[256,512]{1,0:T(8,128)(2,1)}) %reduce-scatter.11.cloned.1.call-update) | async-done | bytes 262160 | tf_op jit(solution)/shard_map/reduce_scatter | solution.py:142
  548.5 75.2 %psum.7 = f32[52,128]{1,0:T(8,128)S(1)} all-reduce(f32[52,128]{1,0:T(8,128)S(1)} %maximum_bitcast_fusion), channel_id=1, replica_groups=mesh['dp'=4,'row'=4,'col'=2] {'row','dp'}, use_global_device_ids=true, to_apply=%region_23.24 | all-reduce | flops 6656 | bytes 53248 | tf_op jit(solution)/shard_map/psum | solution.py:261
  628.9 8.3 %all_gather.29 = bf16[256,512]{1,0:T(8,128)(2,1)S(1)} all-gather(bf16[64,512]{1,0:T(8,128)(2,1)} %reduce-scatter.7.cloned.1.call-done), channel_id=1, replica_groups=mesh['dp'=4,'row'=4,'col'=2] {'dp'}, dimensions={0}, use_global_device_ids=true | all-gather | bytes 327680 | tf_op jit(solution)/shard_map/all_gather | solution.py:143
  638.1 122.3 %reduce-scatter.5.cloned.1.call-done = bf16[64,1536]{1,0:T(8,128)(2,1)} async-done(((bf16[1024,1536]{1,0:T(8,128)(2,1)}), bf16[64,1536]{1,0:T(8,128)(2,1)}) %reduce-scatter.5.cloned.1.call-update) | async-done | bytes 196624 | tf_op jit(solution)/shard_map/reduce_scatter | solution.py:142
  760.4 14.7 %all_gather.28 = bf16[256,1536]{1,0:T(8,128)(2,1)S(1)} all-gather(bf16[64,1536]{1,0:T(8,128)(2,1)} %reduce-scatter.5.cloned.1.call-done), channel_id=1, replica_groups=mesh['dp'=4,'row'=4,'col'=2] {'dp'}, dimensions={0}, use_global_device_ids=true | all-gather | bytes 983040 | tf_op jit(solution)/shard_map/all_gather | solution.py:143
  776.3 12.0 %all-gather.15.cloned.1.call-done = bf16[256,2048]{1,0:T(8,128)(2,1)} async-done(((bf16[64,2048]{1,0:T(8,128)(2,1)}), bf16[256,2048]{1,0:T(8,128)(2,1)}) %all-gather.15.cloned.1.call-update) | async-done | bytes 1048592 | tf_op jit(solution)/shard_map/all_gather | solution.py:143
  791.0 25.7 %all-gather.17.cloned.1.call-done = bf16[1024,512]{1,0:T(8,128)(2,1)} async-done(((bf16[256,512]{1,0:T(8,128)(2,1)}), bf16[1024,512]{1,0:T(8,128)(2,1)}) %all-gather.17.cloned.1.call-update) | async-done | bytes 1048592 | tf_op jit(solution)/shard_map/all_gather | solution.py:143
  (246 shorter events, 173.4 us)
Async XLA Ops:
  7.2 62.2 %all-gather.9.cloned.1.call-start = ((), (), s32[]{:S(2)}) async-start(), calls=%async_computation.5 | async-start | bytes 1114112 | tf_op jit(solution)/shard_map/all_gather | solution.py:138
  8.9 130.9 %all-gather.7.cloned.1.call-start = ((), (), s32[]{:S(2)}) async-start(), calls=%async_computation.4 | async-start | bytes 3342336 | tf_op jit(solution)/shard_map/all_gather | solution.py:138
  10.5 207.2 %all-gather.13.cloned.1.call-start = ((), (), s32[]{:S(2)}) async-start(), calls=%async_computation.7 | async-start | bytes 4456448 | tf_op jit(solution)/shard_map/all_gather | solution.py:138
  11.4 283.7 %all-gather.11.cloned.1.call-start = ((), (), s32[]{:S(2)}) async-start(), calls=%async_computation.6 | async-start | bytes 4456448 | tf_op jit(solution)/shard_map/all_gather | solution.py:138
  12.9 132.9 %copy-start.31 = (bf16[1024,512]{0,1:T(8,128)(2,1)}, bf16[1024,512]{0,1:T(8,128)(2,1)S(1)}, u32[]{:S(2)}) copy-start(bf16[1024,512]{0,1:T(8,128)(2,1)S(1)} %copy.76) | copy-start | bytes 3145732
  12.9 58.8 %collective-permute-start = (bf16[1024,512]{0,1:T(8,128)(2,1)S(1)}, bf16[1024,512]{0,1:T(8,128)(2,1)}, u32[]{:S(2)}, u32[]{:S(2)}) collective-permute-start(bf16[1024,512]{0,1:T(8,128)(2,1)S(1)} %copy.76), channel_id=1, source_target_pairs={{0,1},{1,0},{2,3},{3,2},{4,5},{5,4},{6,7},{7,6},{8,9},{9,8},{10,11... | collective-permute-start | bytes 3145736 | tf_op jit(solution)/shard_map/ppermute | solution.py:115
  15.1 475.3 %reduce-scatter.9.cloned.1.call-start = ((), (), s32[]{:S(2)}) async-start(), calls=%async_computation.10 | async-start | bytes 4456448 | tf_op jit(solution)/shard_map/reduce_scatter | solution.py:142
  71.7 150.6 %collective-permute-start.2 = (bf16[1024,512]{0,1:T(8,128)(2,1)}, bf16[1024,512]{0,1:T(8,128)(2,1)}, u32[]{:S(2)}, u32[]{:S(2)}) collective-permute-start(bf16[1024,512]{0,1:T(8,128)(2,1)} %copy.83), channel_id=1, source_target_pairs={{0,1},{1,0},{2,3},{3,2},{4,5},{5,4},{6,7},{7,6},{8,9},{9,8},{10,11... | collective-permute-start | bytes 3145736 | tf_op jit(solution)/shard_map/ppermute | solution.py:115
  191.2 31.1 %copy-start.34 = (bf16[1024,8,64]{0,2,1:T(8,128)(2,1)}, bf16[1024,8,64]{0,2,1:T(8,128)(2,1)S(1)}, u32[]{:S(2)}) copy-start(bf16[1024,8,64]{0,2,1:T(8,128)(2,1)S(1)} %pad_maximum_fusion.1) | copy-start | bytes 3145732
  191.2 31.1 %collective-permute-start.1 = (bf16[1024,512]{0,1:T(8,128)(2,1)S(1)}, bf16[1024,512]{0,1:T(8,128)(2,1)}, u32[]{:S(2)}, u32[]{:S(2)}) collective-permute-start(bf16[1024,512]{0,1:T(8,128)(2,1)S(1)} %bitcast.119), channel_id=1, source_target_pairs={{0,1},{1,0},{2,3},{3,2},{4,5},{5,4},{6,7},{7,6},{8,9},{9,8},{10,11... | collective-permute-start | bytes 3145736 | tf_op jit(solution)/shard_map/ppermute | solution.py:115
  191.4 2.5 collective-permute-start.3
  222.2 84.5 %collective-permute-start.4 = (bf16[2048,512]{1,0:T(8,128)(2,1)}, bf16[2048,512]{1,0:T(8,128)(2,1)}, u32[]{:S(2)}, u32[]{:S(2)}) collective-permute-start(bf16[2048,512]{1,0:T(8,128)(2,1)} %get-tuple-element.90), channel_id=1, source_target_pairs={{0,1},{1,0},{2,3},{3,2},{4,5},{5,4},{6,7},{7,6},{8,9},{9,8},{10,11... | collective-permute-start | bytes 6291464 | tf_op jit(solution)/shard_map/ppermute | solution.py:115
  316.7 4.5 collective-permute-start.5
  317.2 8.5 %collective-permute-start.6 = (bf16[1024,512]{0,1:T(8,128)(2,1)S(1)}, bf16[1024,512]{0,1:T(8,128)(2,1)S(1)}, u32[]{:S(2)}, u32[]{:S(2)}) collective-permute-start(bf16[1024,512]{0,1:T(8,128)(2,1)S(1)} %copy.87), channel_id=1, source_target_pairs={{0,1},{1,0},{2,3},{3,2},{4,5},{5,4},{6,7},{7,6},{8,9},{9,8},{10,11... | collective-permute-start | bytes 3145736 | tf_op jit(solution)/shard_map/ppermute | solution.py:115
  357.0 190.8 %reduce-scatter.11.cloned.1.call-start = ((), (), s32[]{:S(2)}) async-start(), calls=%async_computation.12 | async-start | bytes 4456448 | tf_op jit(solution)/shard_map/reduce_scatter | solution.py:142
  366.4 11.7 %collective-permute-start.7 = (bf16[1024,1024]{0,1:T(8,128)(2,1)}, bf16[1024,1024]{0,1:T(8,128)(2,1)}, u32[]{:S(2)}, u32[]{:S(2)}) collective-permute-start(bf16[1024,1024]{0,1:T(8,128)(2,1)} %convolution_convert_fusion.4), channel_id=1, source_target_pairs={{0,1},{1,0},{2,3},{3,2},{4,5},{5,4},{6,7},{7,6},{8,9},{9,8},{10,11... | collective-permute-start | bytes 6291464 | tf_op jit(solution)/shard_map/ppermute | solution.py:115
  377.9 15.3 %collective-permute-start.9 = (bf16[2048,512]{1,0:T(8,128)(2,1)S(1)}, bf16[2048,512]{1,0:T(8,128)(2,1)S(1)}, u32[]{:S(2)}, u32[]{:S(2)}) collective-permute-start(bf16[2048,512]{1,0:T(8,128)(2,1)S(1)} %get-tuple-element.88), channel_id=1, source_target_pairs={{0,1},{1,0},{2,3},{3,2},{4,5},{5,4},{6,7},{7,6},{8,9},{9,8},{10,11... | collective-permute-start | bytes 6291464 | tf_op jit(solution)/shard_map/ppermute | solution.py:115
  396.0 232.9 %reduce-scatter.7.cloned.1.call-start = ((), (), s32[]{:S(2)}) async-start(), calls=%async_computation.9 | async-start | bytes 1114112 | tf_op jit(solution)/shard_map/reduce_scatter | solution.py:142
  468.7 291.7 %reduce-scatter.5.cloned.1.call-start = ((), (), s32[]{:S(2)}) async-start(), calls=%async_computation.8 | async-start | bytes 3342336 | tf_op jit(solution)/shard_map/reduce_scatter | solution.py:142
  490.4 297.8 %all-gather.15.cloned.1.call-start = ((), (), s32[]{:S(2)}) async-start(), calls=%async_computation.11 | async-start | bytes 1310720 | tf_op jit(solution)/shard_map/all_gather | solution.py:143
  491.1 325.6 %all-gather.17.cloned.1.call-start = ((), (), s32[]{:S(2)}) async-start(), calls=%async_computation.13 | async-start | bytes 1310720 | tf_op jit(solution)/shard_map/all_gather | solution.py:143
  498.4 49.5 %copy-start.20 = (bf16[1024,8,64]{0,2,1:T(8,128)(2,1)S(1)}, bf16[1024,8,64]{0,2,1:T(8,128)(2,1)}, u32[]{:S(2)}) copy-start(bf16[1024,8,64]{0,2,1:T(8,128)(2,1)} %copy-done.19) | copy-start | bytes 3145732
  499.5 125.4 %collective-permute-start.8 = (bf16[1024,512]{0,1:T(8,128)(2,1)}, bf16[1024,512]{0,1:T(8,128)(2,1)}, u32[]{:S(2)}, u32[]{:S(2)}) collective-permute-start(bf16[1024,512]{0,1:T(8,128)(2,1)} %constant_dynamic-slice_fusion.2), channel_id=1, source_target_pairs={{0,1},{1,0},{2,3},{3,2},{4,5},{5,4},{6,7},{7,6},{8,9},{9,8},{10,11... | collective-permute-start | bytes 3145736 | tf_op jit(solution)/shard_map/ppermute | solution.py:115
  760.4 59.2 %copy-start.1 = (bf16[1024,512]{1,0:T(8,128)(2,1)S(1)}, bf16[1024,512]{1,0:T(8,128)(2,1)}, u32[]{:S(2)}) copy-start(bf16[1024,512]{1,0:T(8,128)(2,1)} %param.30) | copy-start | bytes 3145732
  (57 other events, 472.1 us)
Sparse Core Ops, SparseCore 0:
  11.4 57.9 all-gather.8
  72.8 66.9 all-gather.6
  143.1 74.5 all-gather.12
  220.3 74.6 all-gather.10
  357.1 93.7 reduce-scatter.8
  453.1 94.7 reduce-scatter.10
  550.1 77.3 reduce-scatter.6
  633.3 127.0 reduce-scatter.4
  762.4 25.8 all-gather.14
  790.1 26.6 all-gather.16

commit v2 on v1

v2 whole, which is shorter than its diff:
```python
import jax
import jax.numpy as jnp
from jax import lax
from jax.experimental import pallas as pl
from jax.experimental.pallas import tpu as pltpu
from jax.sharding import PartitionSpec as P

HEAD_DIM = 64


EPSILON = 1e-05
SCALE = 0.125
LOG2E = 1.4426950408889634
PAIR = 2 * HEAD_DIM
Q_BLOCK = 256


def dot_nt(left, right):
    return lax.dot_general(
        left, right, (((1,), (1,)), ((), ())), preferred_element_type=jnp.float32
    )


def dot_nn(left, right):
    return lax.dot_general(
        left, right, (((1,), (0,)), ((), ())), preferred_element_type=jnp.float32
    )


def only_head(block, head):
    lane = lax.broadcasted_iota(jnp.int32, block.shape, 1)
    return jnp.where(lane // HEAD_DIM == head, block, jnp.zeros_like(block))


def attend_kernel(seg_col, seg_row, q_ref, k_ref, v_ref, ctx_ref, lse_ref, vt_ref):
    @pl.when(pl.program_id(1) == 0)
    def _():
        vt_ref[...] = v_ref[...].T

    same = seg_col[...] == seg_row[...]
    parts = []
    for head in range(2):
        scores = dot_nt(k_ref[...], only_head(q_ref[...], head)) * (SCALE * LOG2E)
        scores = jnp.where(same, scores, -1e30)
        top = jnp.max(scores, axis=0, keepdims=True)
        expo = jnp.exp2(scores - top)
        total = jnp.sum(expo, axis=0, keepdims=True)
        out = dot_nn(
            vt_ref[head * HEAD_DIM : (head + 1) * HEAD_DIM, :], expo.astype(jnp.bfloat16)
        )
        parts.append(out / total)
        lse_ref[0, head : head + 1, :] = top + jnp.log2(total)
    ctx_ref[...] = jnp.concatenate(parts, axis=0).T.astype(jnp.bfloat16)


def attend_back_kernel(
    seg_col, seg_row, q_ref, k_ref, v_ref, lse_ref, do_ref, dq_ref, dk_ref, dv_ref, kt_ref, dk_acc, dv_acc
):
    step = pl.program_id(1)

    @pl.when(step == 0)
    def _():
        kt_ref[...] = k_ref[...].T
        dk_acc[...] = jnp.zeros_like(dk_acc)
        dv_acc[...] = jnp.zeros_like(dv_acc)

    same = seg_col[...] == seg_row[...]
    parts = []
    for head in range(2):
        query = only_head(q_ref[...], head)
        grad = only_head(do_ref[...], head)
        scores = dot_nt(k_ref[...], query) * (SCALE * LOG2E)
        probs = jnp.where(same, jnp.exp2(scores - lse_ref[0, head : head + 1, :]), 0.0)
        d_probs = dot_nt(v_ref[...], grad)
        inner = jnp.sum(probs * d_probs, axis=0, keepdims=True)
        d_scores = (probs * (d_probs - inner)).astype(jnp.bfloat16)
        dv_acc[...] += dot_nn(probs.astype(jnp.bfloat16), grad)
        dk_acc[...] += dot_nn(d_scores, query)
        parts.append(
            dot_nn(kt_ref[head * HEAD_DIM : (head + 1) * HEAD_DIM, :], d_scores)
        )
    dq_ref[...] = (jnp.concatenate(parts, axis=0) * SCALE).T.astype(jnp.bfloat16)

    @pl.when(step == pl.num_programs(1) - 1)
    def _():
        dk_ref[...] = (dk_acc[...] * SCALE).astype(jnp.bfloat16)
        dv_ref[...] = dv_acc[...].astype(jnp.bfloat16)


def attention_specs(count, pairs, block):
    seg_col = pl.BlockSpec((count, 1), lambda h, i: (0, 0))
    seg_row = pl.BlockSpec((1, block), lambda h, i: (0, i))
    query = pl.BlockSpec((block, PAIR), lambda h, i: (i, h))
    key = pl.BlockSpec((count, PAIR), lambda h, i: (0, pairs + h))
    value = pl.BlockSpec((count, PAIR), lambda h, i: (0, 2 * pairs + h))
    lse = pl.BlockSpec((1, 2, block), lambda h, i: (h, 0, i))
    return seg_col, seg_row, query, key, value, lse


def attend(qkv, segment):
    count = qkv.shape[0]
    pairs = qkv.shape[1] // (3 * PAIR)
    block = min(Q_BLOCK, count)
    seg_col, seg_row, query, key, value, lse = attention_specs(count, pairs, block)
    return pl.pallas_call(
        attend_kernel,
        grid=(pairs, count // block),
        in_specs=[seg_col, seg_row, query, key, value],
        out_specs=[query, lse],
        out_shape=[
            jax.ShapeDtypeStruct((count, pairs * PAIR), jnp.bfloat16),
            jax.ShapeDtypeStruct((pairs, 2, count), jnp.float32),
        ],
        scratch_shapes=[pltpu.VMEM((PAIR, count), jnp.bfloat16)],
        compiler_params=pltpu.CompilerParams(vmem_limit_bytes=32 << 20),
        cost_estimate=pl.CostEstimate(
            flops=16 * count * count * PAIR * pairs,
            bytes_accessed=10 * count * pairs * PAIR,
            transcendentals=2 * count * count * pairs,
        ),
    )(segment.reshape(-1, 1), segment, qkv, qkv, qkv)


def attend_back(qkv, segment, lse_rows, d_context):
    count = qkv.shape[0]
    pairs = qkv.shape[1] // (3 * PAIR)
    block = min(Q_BLOCK, count)
    seg_col, seg_row, query, key, value, lse = attention_specs(count, pairs, block)
    whole = pl.BlockSpec((count, PAIR), lambda h, i: (0, h))
    shape = jax.ShapeDtypeStruct((count, pairs * PAIR), jnp.bfloat16)
    return pl.pallas_call(
        attend_back_kernel,
        grid=(pairs, count // block),
        in_specs=[seg_col, seg_row, query, key, value, lse, query],
        out_specs=[query, whole, whole],
        out_shape=[shape, shape, shape],
        scratch_shapes=[
            pltpu.VMEM((PAIR, count), jnp.bfloat16),
            pltpu.VMEM((count, PAIR), jnp.float32),
            pltpu.VMEM((count, PAIR), jnp.float32),
        ],
        compiler_params=pltpu.CompilerParams(vmem_limit_bytes=32 << 20),
        cost_estimate=pl.CostEstimate(
            flops=40 * count * count * PAIR * pairs,
            bytes_accessed=20 * count * pairs * PAIR,
            transcendentals=2 * count * count * pairs,
        ),
    )(segment.reshape(-1, 1), segment, qkv, qkv, qkv, lse_rows, d_context)


def matmul(left, right):
    return jnp.dot(left, right, preferred_element_type=jnp.float32)


def matmul_tn(left, right):
    return lax.dot_general(
        left, right, (((0,), (0,)), ((), ())), preferred_element_type=jnp.float32
    )


def matmul_nt(left, right):
    return lax.dot_general(
        left, right, (((1,), (1,)), ((), ())), preferred_element_type=jnp.float32
    )


def column_sum(values):
    return jnp.sum(values.astype(jnp.float32), axis=0)


def swapped(part):
    return lax.ppermute(part, "col", [(0, 1), (1, 0)])


def swapped_rows(part):
    other = swapped(part)
    cut = other.shape[1] // 2
    return jnp.concatenate([other[:, cut:], other[:, :cut]], axis=1).astype(jnp.float32)


def partner(part, axis, bit):
    size = lax.axis_size(axis)
    return lax.ppermute(part, axis, [(i, i ^ bit) for i in range(size)])


def shifted(part, step):
    size = lax.axis_size("row")
    return lax.ppermute(part, "row", [(i, (i + step) % size) for i in range(size)])


def after(values, earlier):
    return lax.optimization_barrier((values, earlier))[0]


def is_small_grid(rows):
    return lax.axis_size("row") == 4 and lax.axis_size("dp") == 4 and rows % 128 == 0


def place_kernel(idx, own, s1, s2, s3, near_x, near_y, far_a, far_b, out, sems):
    quarter = s1.shape[0]
    rows = own.shape[0]
    part = quarter // 2

    def at(step, corner, skip, size):
        start = idx[step] * rows + idx[4 + corner] * quarter + skip
        return out.at[pl.ds(pl.multiple_of(start, part), size), :]

    moves = [(own, out.at[pl.ds(pl.multiple_of(idx[0] * rows, rows), rows), :])]
    for step, ref in ((1, s1), (2, s2), (3, s3)):
        piece = pl.ds((step - 1) * quarter, quarter)
        moves.append((ref, at(step, 0, 0, quarter)))
        moves.append((near_x.at[piece, :], at(step, 1, 0, quarter)))
        moves.append((near_y.at[piece, :], at(step, 2, 0, quarter)))
    moves.append((far_a.at[pl.ds(0, quarter), :], at(1, 3, 0, quarter)))
    moves.append((far_a.at[pl.ds(quarter, part), :], at(2, 3, 0, part)))
    moves.append((far_b.at[pl.ds(0, part), :], at(2, 3, part, part)))
    moves.append((far_b.at[pl.ds(part, quarter), :], at(3, 3, 0, quarter)))
    copies = [
        pltpu.make_async_copy(source, target, sems.at[i])
        for i, (source, target) in enumerate(moves)
    ]
    for copy in copies:
        copy.start()
    for copy in copies:
        copy.wait()


def place(idx, own, *pieces):
    rows, width = own.shape
    return pl.pallas_call(
        place_kernel,
        in_specs=[pl.BlockSpec(memory_space=pltpu.SMEM)]
        + [pl.BlockSpec(memory_space=pl.ANY)] * 8,
        out_specs=pl.BlockSpec(memory_space=pl.ANY),
        out_shape=jax.ShapeDtypeStruct((4 * rows, width), own.dtype),
        scratch_shapes=[pltpu.SemaphoreType.DMA((14,))],
        cost_estimate=pl.CostEstimate(
            flops=0, bytes_accessed=8 * rows * width * 2, transcendentals=0
        ),
    )(idx, own, *pieces)


def whole_weights(blocks):
    core, corner = lax.axis_index("col"), lax.axis_index("dp")
    size = lax.axis_size("row")
    if not all(is_small_grid(block.shape[0]) for block in blocks):
        wholes = []
        for block in blocks:
            rows = block.shape[0] // lax.axis_size("dp")
            part = lax.dynamic_slice_in_dim(block, corner * rows, rows, 0)
            full = lax.all_gather(part, ("row", "dp"), axis=0, tiled=True)
            cut = full.shape[0] // 2
            wholes.append(
                jnp.where(core == 0, full, jnp.concatenate([full[cut:], full[:cut]], axis=0))
            )
        return wholes
    place_z = (lax.axis_index("row") + size // 2 * core + size - jnp.arange(size)) % size
    idx = jnp.concatenate([place_z, corner ^ jnp.arange(4)]).astype(jnp.int32)
    wholes = []
    earlier_z = earlier_xy = None
    for block in blocks:
        quarter = block.shape[0] // 4
        part = lax.dynamic_slice_in_dim(block, corner * quarter, quarter, 0)
        if earlier_z is not None:
            part = after(part, earlier_z)
        ring = [shifted(part, step) for step in (1, 2, 3)]
        earlier_z = ring[0]
        stack = jnp.concatenate(ring, axis=0)
        if earlier_xy is not None:
            stack = after(stack, earlier_xy)
        near_x = partner(stack, "dp", 1)
        near_y = partner(stack, "dp", 2)
        cut = stack.shape[0] // 2
        far_a = partner(near_y[:cut], "dp", 1)
        far_b = partner(near_x[cut:], "dp", 2)
        earlier_xy = near_x
        wholes.append(place(idx, block, *ring, near_x, near_y, far_a, far_b))
    return wholes


def pick(values, axis, index):
    return lax.dynamic_index_in_dim(values, index, axis, keepdims=False)


def added(*parts):
    total = parts[0].astype(jnp.float32)
    for part in parts[1:]:
        total = total + part.astype(jnp.float32)
    return total.astype(jnp.bfloat16)


def reduced_weight(grad):
    core, corner, level = lax.axis_index("col"), lax.axis_index("dp"), lax.axis_index("row")
    size = lax.axis_size("row")
    if not is_small_grid(grad.shape[0] // size):
        cut = grad.shape[0] // 2
        grad = jnp.where(core == 0, grad, jnp.concatenate([grad[cut:], grad[:cut]], axis=0))
        part = lax.psum_scatter(grad, ("row", "dp"), scatter_dimension=0, tiled=True)
        return lax.all_gather(part, "dp", axis=0, tiled=True).astype(jnp.float32)
    a, b = corner // 2, corner % 2
    width = grad.shape[1]
    six = grad.reshape(2, 2, 2, 2, -1, width)
    first, second = six[0], six[1]
    got_first = partner(pick(first, 2, 1 - b), "dp", 1)
    got_second = partner(pick(second, 1, 1 - a), "dp", 2)
    send_first = added(pick(pick(first, 2, b), 1, 1 - a), pick(got_first, 1, 1 - a))
    send_second = added(pick(pick(second, 1, a), 1, 1 - b), pick(got_second, 1, 1 - b))
    far_first = partner(send_first, "dp", 2)
    far_second = partner(send_second, "dp", 1)
    keep_first = added(pick(pick(first, 2, b), 1, a), pick(got_first, 1, a), far_first)
    keep_second = added(pick(pick(second, 1, a), 1, b), pick(got_second, 1, b), far_second)
    levels = jnp.concatenate([keep_first, keep_second], axis=0)

    def of_level(index):
        return pick(levels, 0, (index + size // 2 * core) % size)

    total = added(
        of_level(level), *[shifted(of_level((level + step) % size), step) for step in (1, 2, 3)]
    )
    others = [total] + [partner(total, "dp", bit) for bit in (1, 2, 3)]
    return jnp.concatenate(
        [
            jnp.where(
                a == 0,
                jnp.where(b == 0, others[k], others[k ^ 1]),
                jnp.where(b == 0, others[k ^ 2], others[k ^ 3]),
            )
            for k in range(4)
        ],
        axis=0,
    ).astype(jnp.float32)


def reduced_vector(values):
    values = values.reshape(-1, 128)
    if not is_small_grid(128):
        return lax.psum(values, ("row", "dp")).reshape(-1)
    for axis in ("dp", "row"):
        for bit in (1, 2):
            values = values + partner(values, axis, bit)
    return values.reshape(-1)


def norm_forward(resid, gain, shift):
    center = jnp.mean(resid, axis=1, keepdims=True)
    inverse = lax.rsqrt(
        jnp.mean(resid * resid, axis=1, keepdims=True) - center * center + EPSILON
    )
    normed = (resid - center) * inverse
    return (normed * gain + shift, normed, inverse)


def norm_backward(grad, normed, inverse, gain):
    scaled = grad * gain
    first = jnp.mean(scaled, axis=1, keepdims=True)
    second = jnp.mean(scaled * normed, axis=1, keepdims=True)
    return inverse * (scaled - first - normed * second)


def body(
    tokens,
    segment,
    cotangent,
    w_query,
    b_query,
    w_key,
    w_value,
    b_value,
    w_out,
    b_out,
    w_up,
    b_up,
    w_down,
    b_down,
    gain_one,
    shift_one,
    gain_two,
    shift_two,
):
    half = w_query.shape[1]
    token_rows = jnp.concatenate([tokens, swapped(tokens)], axis=1)
    w_qkv, wo_half, wu, wd_half = whole_weights(
        [jnp.concatenate([w_query, w_key, w_value], axis=1), w_out, w_up, w_down]
    )
    cotangent_rows = jnp.concatenate([cotangent, swapped(cotangent)], axis=1)
    own_vectors = jnp.stack([b_out, b_down, gain_one, shift_one, gain_two, shift_two])
    vectors = jnp.concatenate([own_vectors, swapped(own_vectors)], axis=1).astype(jnp.float32)
    bias_out, bias_down, gain1, shift1, gain2, shift2 = [vectors[i] for i in range(6)]
    wo_other = swapped(wo_half)
    wo = jnp.concatenate(
        [wo_half, jnp.concatenate([wo_other[half:], wo_other[:half]], axis=0)], axis=1
    )
    units = w_up.shape[1]
    wd = jnp.concatenate([wd_half[:units], swapped(wd_half[units:])], axis=1)

    b_qkv = jnp.concatenate([b_query, jnp.zeros_like(b_query), b_value]).astype(jnp.float32)
    qkv = (matmul(token_rows, w_qkv) + b_qkv).astype(jnp.bfloat16)
    context, lse_rows = attend(qkv, segment)
    context_rows = jnp.concatenate([context, swapped(context)], axis=1)
    first_sum = token_rows.astype(jnp.float32) + (matmul(context_rows, wo) + bias_out)
    hidden_f, normed_one, inverse_one = norm_forward(first_sum, gain1, shift1)
    hidden = hidden_f.astype(jnp.bfloat16)
    pre_act = matmul(hidden, wu) + b_up.astype(jnp.float32)
    cdf = 0.5 * (1.0 + lax.erf(pre_act * (0.5**0.5)))
    activated = (pre_act * cdf).astype(jnp.bfloat16)
    slope = cdf + pre_act * (jnp.exp(-0.5 * pre_act * pre_act) * 0.3989422804014327)
    part = matmul(activated, wd).astype(jnp.bfloat16)
    ffn_out = part.astype(jnp.float32) + swapped_rows(part) + bias_down
    second_sum = hidden.astype(jnp.float32) + ffn_out
    final, normed_two, inverse_two = norm_forward(second_sum, gain2, shift2)
    output = final[:, :half].astype(jnp.bfloat16)
    y = cotangent_rows.astype(jnp.float32)
    second_grad = norm_backward(y, normed_two, inverse_two, gain2)
    d_gain_two = jnp.sum(y * normed_two, axis=0)
    d_shift_two = jnp.sum(y, axis=0)
    ffn_grad = second_grad.astype(jnp.bfloat16)
    d_w_down = matmul_tn(activated, ffn_grad).astype(jnp.bfloat16)
    o_w_down = reduced_weight(
        jnp.concatenate([d_w_down[:, :half], swapped(d_w_down[:, half:])], axis=0)
    )
    d_b_down = column_sum(ffn_grad)
    pre_grad = (matmul_nt(ffn_grad, wd) * slope).astype(jnp.bfloat16)
    o_w_up = reduced_weight(matmul_tn(hidden, pre_grad).astype(jnp.bfloat16))
    d_b_up = column_sum(pre_grad)
    hidden_part = matmul_nt(pre_grad, wu).astype(jnp.bfloat16)
    hidden_grad = second_grad + (
        hidden_part.astype(jnp.float32) + swapped_rows(hidden_part)
    )
    first_grad = norm_backward(hidden_grad, normed_one, inverse_one, gain1)
    d_gain_one = jnp.sum(hidden_grad * normed_one, axis=0)
    d_shift_one = jnp.sum(hidden_grad, axis=0)
    branch_grad = first_grad.astype(jnp.bfloat16)
    o_w_out = reduced_weight(matmul_tn(context_rows, branch_grad[:, :half]).astype(jnp.bfloat16))
    d_b_out = column_sum(branch_grad)
    wide = jnp.stack([d_b_out, d_b_down, d_gain_one, d_shift_one, d_gain_two, d_shift_two])
    sums = reduced_vector(jnp.concatenate([wide[:, :half].reshape(-1), d_b_up]))
    context_grad = matmul_nt(branch_grad, wo[:half]).astype(jnp.bfloat16)
    qkv_grad = jnp.concatenate(attend_back(qkv, segment, lse_rows, context_grad), axis=1)
    o_w_qkv = reduced_weight(matmul_tn(token_rows, qkv_grad).astype(jnp.bfloat16))
    d_b_qkv = column_sum(qkv_grad)
    d_b_qv = reduced_vector(jnp.concatenate([d_b_qkv[:half], d_b_qkv[2 * half :]]))
    token_part = matmul_nt(qkv_grad, w_qkv).astype(jnp.bfloat16)
    token_sum = token_part[:, :half].astype(jnp.float32) + swapped(
        token_part[:, half:]
    ).astype(jnp.float32)
    d_tokens = (token_sum + first_grad[:, :half]).astype(jnp.bfloat16)
    pieces = [sums[i * half : (i + 1) * half] for i in range(6)]
    return (
        output,
        d_tokens,
        o_w_qkv[:, :half],
        d_b_qv[:half],
        o_w_qkv[:, half : 2 * half],
        o_w_qkv[:, 2 * half :],
        d_b_qv[half:],
        o_w_out,
        pieces[0],
        o_w_up,
        sums[6 * half :],
        o_w_down,
        pieces[1],
        pieces[2],
        pieces[3],
        pieces[4],
        pieces[5],
    )


def solution(mesh):
    in_specs = (
        P(("dp", "row"), "col"),
        P(("dp", "row"), None),
        P(("dp", "row"), "col"),
        P("row", "col"),
        P("col"),
        P("row", "col"),
        P("row", "col"),
        P("col"),
        P("row", "col"),
        P("col"),
        P("row", "col"),
        P("col"),
        P("row", "col"),
        P("col"),
        P("col"),
        P("col"),
        P("col"),
        P("col"),
    )
    out_specs = (
        P(("dp", "row"), "col"),
        P(("dp", "row"), "col"),
        P("row", "col"),
        P("col"),
        P("row", "col"),
        P("row", "col"),
        P("col"),
        P("row", "col"),
        P("col"),
        P("row", "col"),
        P("col"),
        P("row", "col"),
        P("col"),
        P("col"),
        P("col"),
        P("col"),
        P("col"),
    )
    return jax.shard_map(body, mesh=mesh, in_specs=in_specs, out_specs=out_specs, check_vma=False)
```

time: 836 us -> 951 us (1.14)
  Pallas kernels: 0 us -> 452 us
  waiting for transfers between devices: 420 us -> 214 us
  starting transfers between devices: 2.84 us -> 104 us
  blocking collectives: 98.1 us -> 0 us
  matrix products: 168 us -> 78 us
  other arithmetic: 79.9 us -> 45.6 us
  between operations: 15.3 us -> 2.35 us
    pallas_call x0 -> x6, Pallas kernels: none -> 452 us  [the longest x4 389 us: place(): pl.pallas_call(place_kernel, in_specs=[pl.BlockSpec(memory_space=pltpu.SM...]
    all_gather x6 -> x0, waiting for transfers between devices: 247 us -> none  [the longest x4 209 us: whole_weight(): return lax.all_gather(part, ('row', 'dp'), axis=0, tiled=True)]
    ppermute x0 -> x76, waiting for transfers between devices: none -> 211 us  [the longest x52 156 us: partner(): return lax.ppermute(part, axis, [(i, i ^ bit) for i in range(size)])]
    reduce_scatter x4 -> x0, waiting for transfers between devices: 167 us -> none  [reduced_weight(): lax.psum_scatter(grad, ('row', 'dp'), scatter_dimension=0, tiled=True)]
    ppermute x0 -> x76, starting transfers between devices: none -> 102 us  [the longest x52 54.7 us: partner(): return lax.ppermute(part, axis, [(i, i ^ bit) for i in range(size)])]
    dot_general x12 -> x0, matrix products: 77.6 us -> none  [the longest x2 20.7 us: attend_back(): jnp.einsum('qhd,khd->hqk', grad_block, value_three, preferred_element_typ...]
    psum x1 -> x0, blocking collectives: 75.2 us -> none  [body(): lax.psum(jnp.concatenate([wide.reshape(-1), d_b_qkv, d_b_up]).reshape(-1,...]
    all_gather x2 -> x0, blocking collectives: 22.9 us -> none  [reduced_weight(): return lax.all_gather(part, 'dp', axis=0, tiled=True).astype(jnp.float32)]
  transfers between devices with their start and end apart: 20 -> 86, of which waited for: 10 -> 34; matrix products, arithmetic and copies ran while one was open for 28% -> 13% of each run, Pallas kernels for 0% -> 48%
where the time goes in v2:
time: 951 us; the launch traced here: 942 us
  Pallas kernels  452 us (48%)
  waiting for transfers between devices  214 us (23%)
  starting transfers between devices  104 us (11%)
  matrix products  78 us (8%)
  local copies, waits for them, and re-layouts  46.8 us (5%)
  other arithmetic  45.6 us (5%)
    pallas_call x4, Pallas kernels, place(): pl.pallas_call(place_kernel, in_specs=[pl.BlockSpec(memory_space=pltpu.SM...  389 us
    ppermute x52, waiting for transfers between devices, partner(): return lax.ppermute(part, axis, [(i, i ^ bit) for i in range(size)])  156 us
    ppermute x24, waiting for transfers between devices, shifted(): lax.ppermute(part, 'row', [(i, (i + step) % size) for i in range(size)])  55.7 us
    ppermute x52, starting transfers between devices, partner(): return lax.ppermute(part, axis, [(i, i ^ bit) for i in range(size)])  54.7 us
    ppermute x24, starting transfers between devices, shifted(): lax.ppermute(part, 'row', [(i, (i + step) % size) for i in range(size)])  47.6 us
    dot_general x4, matrix products, matmul(): return jnp.dot(left, right, preferred_element_type=jnp.float32)  36.1 us
    pallas_call x1, Pallas kernels, attend_back(): pl.pallas_call(attend_back_kernel, grid=(pairs, count // block), in_specs...  34.9 us
    pallas_call x1, Pallas kernels, attend(): pl.pallas_call(attend_kernel, grid=(pairs, count // block), in_specs=[seg...  27.9 us
  transfers between devices with their start and end apart: 86, of which 34 were waited for; matrix products, arithmetic and copies ran while one was open for 13% of the time, Pallas kernels for 48%

profile of v2, /device:TPU:0, one launch (start us, length us, event | category | flops | bytes accessed | tf_op | source)
XLA Modules:
  0.0 941.8 jit_solution(13782455827970953338)
XLA Ops:
  15.4 6.8 collective-permute-done.2.s2
  50.4 12.5 %collective-permute-done.11.s3 = bf16[64,512]{1,0:T(8,128)(2,1)S(1)} collective-permute-done((bf16[64,512]{1,0:T(8,128)(2,1)}, bf16[64,512]{1,0:T(8,128)(2,1)S(1)}, u32[]{:S(2)}, u32[]{:S(2)}) %collective-permute-start.11) | collective-permute-done | bytes 65568 | tf_op jit(solution)/shard_map/ppermute | solution.py:188
  68.0 8.0 collective-permute-done.12.near_x
  76.0 6.5 collective-permute-start.25
  87.0 97.2 %shard_map.305 = bf16[1024,1536]{1,0:T(8,128)(2,1)} custom-call(s32[8]{0:T(128)} %pad_add_fusion.idx, bf16[256,1536]{1,0:T(8,128)(2,1)} %copy-done.19, bf16[64,1536]{1,0:T(8,128)(2,1)} %copy-done.32, bf16[64,1536]{1,0:T(8,128)(2,1)} %copy-done.33, bf16[64,1536]{1,0:T(8,128)(2,1)} %copy-done.34, bf16[192,1536]{1,0:T(8,128)(2,1)} %copy-done.24, ...), custom_call_target="tpu_custom_call" | custom-call | bytes 6291456 | tf_op jit(solution)/shard_map/pallas_call | solution.py:230
  193.5 27.9 %shard_map.306 = (bf16[1024,512]{1,0:T(8,128)(2,1)S(1)}, f32[4,2,1024]{2,1,0:T(2,128)S(1)}) custom-call(s32[1024,1]{1,0:T(8,128)S(1)} %copy.70.seg_col, s32[1,1024]{1,0:T(1,128)S(1)} %copy-done, bf16[1024,1536]{1,0:T(8,128)(2,1)S(1)} %add_convert_fusion.q_ref.k_ref.v_ref, bf16[1024,1536]{1,0:T(8,128)(2,1)S(1)} %add_convert_fusion.q_ref.k_ref.v_ref, ...), custom_call_target="tpu_custom_call" | custom-call | flops 8589934592 | bytes 5242880 | tf_op jit(solution)/shard_map/pallas_call | solution.py:105
  222.1 33.7 %shard_map.307 = bf16[1024,512]{1,0:T(8,128)(2,1)} custom-call(s32[8]{0:T(128)} %pad_add_fusion.idx, bf16[256,512]{1,0:T(8,128)(2,1)} %own.3, bf16[64,512]{1,0:T(8,128)(2,1)} %copy-done.49, bf16[64,512]{1,0:T(8,128)(2,1)} %copy-done.50, bf16[64,512]{1,0:T(8,128)(2,1)} %copy-done.51, bf16[192,512]{1,0:T(8,128)(2,1)} %copy-done.42, ...), custom_call_target="tpu_custom_call" | custom-call | bytes 2097152 | tf_op jit(solution)/shard_map/pallas_call | solution.py:230
  260.3 17.8 %collective-permute-done.22.near_y = bf16[192,2048]{1,0:T(8,128)(2,1)S(1)} collective-permute-done((bf16[192,2048]{1,0:T(8,128)(2,1)}, bf16[192,2048]{1,0:T(8,128)(2,1)S(1)}, u32[]{:S(2)}, u32[]{:S(2)}) %collective-permute-start.22) | collective-permute-done | bytes 786464 | tf_op jit(solution)/shard_map/ppermute | solution.py:183
  280.3 13.9 %collective-permute-done.29.near_y = bf16[768,512]{1,0:T(8,128)(2,1)S(1)} collective-permute-done((bf16[768,512]{1,0:T(8,128)(2,1)S(1)}, bf16[768,512]{1,0:T(8,128)(2,1)S(1)}, u32[]{:S(2)}, u32[]{:S(2)}) %collective-permute-start.29) | collective-permute-done | bytes 786464 | tf_op jit(solution)/shard_map/ppermute | solution.py:183
  305.6 7.5 collective-permute-done.31.far_b
  313.9 128.9 %shard_map.309 = bf16[4096,512]{1,0:T(8,128)(2,1)} custom-call(s32[8]{0:T(128)} %pad_add_fusion.idx, bf16[1024,512]{1,0:T(8,128)(2,1)} %own.5, bf16[256,512]{1,0:T(8,128)(2,1)} %collective-permute-done.25.s1, bf16[256,512]{1,0:T(8,128)(2,1)} %collective-permute-done.26.s2, bf16[256,512]{1,0:T(8,128)(2,1)} %collective-permute-done.27.s3, ...), custom_call_target="tpu_custom_call" | custom-call | bytes 8388608 | tf_op jit(solution)/shard_map/pallas_call | solution.py:230
  446.9 10.1 %fusion.112 = (f32[1024]{0:T(1024)S(1)}, f32[1024]{0:T(1024)S(1)}, f32[1024,1024]{0,1:T(8,128)}) fusion(f32[1024]{0:T(1024)S(1)} %bitcast.302, bf16[1024,1024]{1,0:T(8,128)(2,1)S(1)} %copy-done.36, bf16[512,512]{1,0:T(8,128)(2,1)S(1)} %copy-done.40, bf16[512,512]{1,0:T(8,128)(2,1)S(1)} %copy-done.38, bf16[1024,512]{1,0:T(8,128)(2,1)S(1)} %copy-done.26, ...), kind=kOutput, calls=%fused_computation.300 | convolution fusion | flops 2163210240 | bytes 10498048 | tf_op jit(solution)/shard_map/dot_general | solution.py:152
  457.0 129.0 %shard_map.308 = bf16[1024,2048]{1,0:T(8,128)(2,1)} custom-call(s32[8]{0:T(128)} %pad_add_fusion.idx, bf16[256,2048]{1,0:T(8,128)(2,1)} %own.4, bf16[64,2048]{1,0:T(8,128)(2,1)} %copy-done.29, bf16[64,2048]{1,0:T(8,128)(2,1)} %copy-done.30, bf16[64,2048]{1,0:T(8,128)(2,1)} %copy-done.31, bf16[192,2048]{1,0:T(8,128)(2,1)} %copy-done.20, ...), custom_call_target="tpu_custom_call" | custom-call | bytes 8388608 | tf_op jit(solution)/shard_map/pallas_call | solution.py:230
  586.0 11.1 %multiply_convert_fusion = (bf16[1024,2048]{1,0:T(8,128)(2,1)S(1)}, f32[1024,2048]{1,0:T(8,128)}) fusion(f32[2048]{0:T(1024)S(1)} %convert_element_type.452, bf16[1024,2048]{1,0:T(8,128)(2,1)} %shard_map.308, f32[1024,1024]{0,1:T(8,128)} %get-tuple-element.159, f32[1024]{0:T(1024)S(1)} %bitcast.289, f32[1024]{0:T(1024)S(1)} %bitcast.279, ...), kind=kOutput, calls=%fused_computation.8 | convolution fusion | flops 4312793088 | bytes 20996096 | tf_op jit(solution)/shard_map/dot_general | solution.py:152
  597.1 8.9 fusion.23
  625.8 10.0 %convert_reduce_fusion = (f32[2048]{0:T(1024)S(1)}, bf16[1024,2048]{1,0:T(8,128)(2,1)}) fusion(f32[1024,2048]{1,0:T(8,128)S(1)} %bitcast.304, f32[2048]{0:T(1024)S(1)} %convert_element_type.452, bf16[1024,1024]{0,1:T(8,128)(2,1)S(1)} %get-tuple-element.86, bf16[2048,512]{1,0:T(8,128)(2,1)} %collective-permute-done.32, bf16[2048,512]{1,0:T(8,128)(2,1)S(1)} %copy-done.18), kind=kOutput, calls=%fused_computation.7 | convolution fusion | flops 4330616832 | bytes 18890752 | tf_op jit(solution)/shard_map/dot_general | solution.py:162
  635.8 7.3 convolution_convert_fusion.2
  654.7 14.1 %collective-permute-done.67 = bf16[2,2,64,2048]{3,2,0,1:T(8,128)(2,1)S(1)} collective-permute-done((bf16[2,2,64,2048]{3,2,0,1:T(8,128)(2,1)S(1)}, bf16[2,2,64,2048]{3,2,0,1:T(8,128)(2,1)S(1)}, u32[]{:S(2)}, u32[]{:S(2)}) %collective-permute-start.67) | collective-permute-done | bytes 1048608 | tf_op jit(solution)/shard_map/ppermute | solution.py:183
  675.3 25.7 %collective-permute-done.65 = bf16[2,2,64,2048]{3,2,0,1:T(8,128)(2,1)S(1)} collective-permute-done((bf16[2,2,64,2048]{3,2,0,1:T(8,128)(2,1)S(1)}, bf16[2,2,64,2048]{3,2,0,1:T(8,128)(2,1)S(1)}, u32[]{:S(2)}, u32[]{:S(2)}) %collective-permute-start.65) | collective-permute-done | bytes 1048608 | tf_op jit(solution)/shard_map/ppermute | solution.py:183
  703.4 8.0 collective-permute-done.68
  753.1 34.9 %shard_map.310 = (bf16[1024,512]{1,0:T(8,128)(2,1)S(1)}, bf16[1024,512]{1,0:T(8,128)(2,1)S(1)}, bf16[1024,512]{1,0:T(8,128)(2,1)S(1)}) custom-call(s32[1024,1]{1,0:T(8,128)S(1)} %copy.70.seg_col, s32[1,1024]{1,0:T(1,128)S(1)} %copy-done, bf16[1024,1536]{1,0:T(8,128)(2,1)S(1)} %copy-done.2, bf16[1024,1536]{1,0:T(8,128)(2,1)S(1)} %copy-done.2, ...), custom_call_target="tpu_custom_call" | custom-call | flops 21474836480 | bytes 10485760 | tf_op jit(solution)/shard_map/pallas_call | solution.py:131
  818.3 9.4 collective-permute-done.48
  858.1 10.3 %collective-permute-done.58 = bf16[64,512]{1,0:T(8,128)(2,1)S(1)} collective-permute-done((bf16[64,512]{1,0:T(8,128)(2,1)S(1)}, bf16[64,512]{1,0:T(8,128)(2,1)S(1)}, u32[]{:S(2)}, u32[]{:S(2)}) %collective-permute-start.58) | collective-permute-done | bytes 65568 | tf_op jit(solution)/shard_map/ppermute | solution.py:183
  917.8 7.2 collective-permute-done.81
  (432 shorter events, 292.6 us)
Async XLA Ops:
  28.0 156.2 %collective-permute-start = (bf16[1024,512]{0,1:T(8,128)(2,1)}, bf16[1024,512]{0,1:T(8,128)(2,1)}, u32[]{:S(2)}, u32[]{:S(2)}) collective-permute-start(bf16[1024,512]{0,1:T(8,128)(2,1)} %copy.69), channel_id=1, source_target_pairs={{0,1},{1,0},{2,3},{3,2},{4,5},{5,4},{6,7},{7,6},{8,9},{9,8},{10,11... | collective-permute-start | bytes 3145736 | tf_op jit(solution)/shard_map/ppermute | solution.py:172
  76.0 179.7 %collective-permute-start.25 = (bf16[256,512]{1,0:T(8,128)(2,1)}, bf16[256,512]{1,0:T(8,128)(2,1)}, u32[]{:S(2)}, u32[]{:S(2)}) collective-permute-start(bf16[256,512]{1,0:T(8,128)(2,1)} %constant_dynamic-slice_fusion.8), channel_id=1, source_target_pairs={{0,2},{2,4},{4,6},{6,0},{1,3},{3,5},{5,7},{7,1},{8,10},{10,12},{12... | collective-permute-start | bytes 786440 | tf_op jit(solution)/shard_map/ppermute | solution.py:188
  82.6 173.4 %collective-permute-start.26 = (bf16[256,512]{1,0:T(8,128)(2,1)}, bf16[256,512]{1,0:T(8,128)(2,1)}, u32[]{:S(2)}, u32[]{:S(2)}) collective-permute-start(bf16[256,512]{1,0:T(8,128)(2,1)} %constant_dynamic-slice_fusion.8), channel_id=1, source_target_pairs={{0,4},{2,6},{4,0},{6,2},{1,5},{3,7},{5,1},{7,3},{8,12},{10,14},{12... | collective-permute-start | bytes 786440 | tf_op jit(solution)/shard_map/ppermute | solution.py:188
  83.3 173.0 %collective-permute-start.27 = (bf16[256,512]{1,0:T(8,128)(2,1)}, bf16[256,512]{1,0:T(8,128)(2,1)}, u32[]{:S(2)}, u32[]{:S(2)}) collective-permute-start(bf16[256,512]{1,0:T(8,128)(2,1)} %constant_dynamic-slice_fusion.8), channel_id=1, source_target_pairs={{0,6},{2,0},{4,2},{6,4},{1,7},{3,1},{5,3},{7,5},{8,14},{10,8},{12,... | collective-permute-start | bytes 786440 | tf_op jit(solution)/shard_map/ppermute | solution.py:188
  86.4 171.6 %collective-permute-start.21 = (bf16[192,2048]{1,0:T(8,128)(2,1)}, bf16[192,2048]{1,0:T(8,128)(2,1)S(1)}, u32[]{:S(2)}, u32[]{:S(2)}) collective-permute-start(bf16[192,2048]{1,0:T(8,128)(2,1)} %pad_maximum_fusion.7), channel_id=1, source_target_pairs={{0,8},{8,0},{16,24},{24,16},{1,9},{9,1},{17,25},{25,17},{2,10},{10... | collective-permute-start | bytes 2359304 | tf_op jit(solution)/shard_map/ppermute | solution.py:183
  221.5 73.9 %collective-permute-start.8 = (bf16[1024,512]{1,0:T(8,128)(2,1)S(1)}, bf16[1024,512]{1,0:T(8,128)(2,1)}, u32[]{:S(2)}, u32[]{:S(2)}) collective-permute-start(bf16[1024,512]{1,0:T(8,128)(2,1)S(1)} %get-tuple-element.28), channel_id=1, source_target_pairs={{0,1},{1,0},{2,3},{3,2},{4,5},{5,4},{6,7},{7,6},{8,9},{9,8},{10,11... | collective-permute-start | bytes 3145736 | tf_op jit(solution)/shard_map/ppermute | solution.py:172
  255.9 42.4 %collective-permute-start.16 = (bf16[1024,512]{1,0:T(8,128)(2,1)}, bf16[1024,512]{1,0:T(8,128)(2,1)S(1)}, u32[]{:S(2)}, u32[]{:S(2)}) collective-permute-start(bf16[1024,512]{1,0:T(8,128)(2,1)} %shard_map.307), channel_id=1, source_target_pairs={{0,1},{1,0},{2,3},{3,2},{4,5},{5,4},{6,7},{7,6},{8,9},{9,8},{10,11... | collective-permute-start | bytes 3145736 | tf_op jit(solution)/shard_map/ppermute | solution.py:172
  258.1 36.1 %collective-permute-start.29 = (bf16[768,512]{1,0:T(8,128)(2,1)S(1)}, bf16[768,512]{1,0:T(8,128)(2,1)S(1)}, u32[]{:S(2)}, u32[]{:S(2)}) collective-permute-start(bf16[768,512]{1,0:T(8,128)(2,1)S(1)} %pad_maximum_fusion.8), channel_id=1, source_target_pairs={{0,16},{8,24},{16,0},{24,8},{1,17},{9,25},{17,1},{25,9},{2,18},{10... | collective-permute-start | bytes 2359304 | tf_op jit(solution)/shard_map/ppermute | solution.py:183
  259.6 35.1 %collective-permute-start.28 = (bf16[768,512]{1,0:T(8,128)(2,1)S(1)}, bf16[768,512]{1,0:T(8,128)(2,1)S(1)}, u32[]{:S(2)}, u32[]{:S(2)}) collective-permute-start(bf16[768,512]{1,0:T(8,128)(2,1)S(1)} %pad_maximum_fusion.8), channel_id=1, source_target_pairs={{0,8},{8,0},{16,24},{24,16},{1,9},{9,1},{17,25},{25,17},{2,10},{10... | collective-permute-start | bytes 2359304 | tf_op jit(solution)/shard_map/ppermute | solution.py:183
  279.0 178.0 %collective-permute-start.23 = (bf16[96,2048]{1,0:T(8,128)(2,1)}, bf16[96,2048]{1,0:T(8,128)(2,1)}, u32[]{:S(2)}, u32[]{:S(2)}) collective-permute-start(bf16[96,2048]{1,0:T(8,128)(2,1)} %slice.279), channel_id=1, source_target_pairs={{0,8},{8,0},{16,24},{24,16},{1,9},{9,1},{17,25},{25,17},{2,10},{10... | collective-permute-start | bytes 1179656 | tf_op jit(solution)/shard_map/ppermute | solution.py:183
  294.2 162.8 %collective-permute-start.24 = (bf16[96,2048]{1,0:T(8,128)(2,1)}, bf16[96,2048]{1,0:T(8,128)(2,1)}, u32[]{:S(2)}, u32[]{:S(2)}) collective-permute-start(bf16[96,2048]{1,0:T(8,128)(2,1)} %slice.280), channel_id=1, source_target_pairs={{0,16},{8,24},{16,0},{24,8},{1,17},{9,25},{17,1},{25,9},{2,18},{10... | collective-permute-start | bytes 1179656 | tf_op jit(solution)/shard_map/ppermute | solution.py:183
  446.9 150.2 %collective-permute-start.32 = (bf16[2048,512]{1,0:T(8,128)(2,1)}, bf16[2048,512]{1,0:T(8,128)(2,1)}, u32[]{:S(2)}, u32[]{:S(2)}) collective-permute-start(bf16[2048,512]{1,0:T(8,128)(2,1)} %get-tuple-element.97), channel_id=1, source_target_pairs={{0,1},{1,0},{2,3},{3,2},{4,5},{5,4},{6,7},{7,6},{8,9},{9,8},{10,11... | collective-permute-start | bytes 6291464 | tf_op jit(solution)/shard_map/ppermute | solution.py:172
  652.5 49.2 %collective-permute-start.75 = (bf16[2,2,256,512]{3,2,0,1:T(8,128)(2,1)S(1)}, bf16[2,2,256,512]{3,2,0,1:T(8,128)(2,1)S(1)}, u32[]{:S(2)}, u32[]{:S(2)}) collective-permute-start(bf16[2,2,256,512]{3,2,0,1:T(8,128)(2,1)S(1)} %copy_bitcast_fusion.1), channel_id=1, source_target_pairs={{0,8},{8,0},{16,24},{24,16},{1,9},{9,1},{17,25},{25,17},{2,10},{10... | collective-permute-start | bytes 3145736 | tf_op jit(solution)/shard_map/ppermute | solution.py:183
  653.1 47.9 %collective-permute-start.65 = (bf16[2,2,64,2048]{3,2,0,1:T(8,128)(2,1)S(1)}, bf16[2,2,64,2048]{3,2,0,1:T(8,128)(2,1)S(1)}, u32[]{:S(2)}, u32[]{:S(2)}) collective-permute-start(bf16[2,2,64,2048]{3,2,0,1:T(8,128)(2,1)S(1)} %copy_bitcast_fusion.3), channel_id=1, source_target_pairs={{0,8},{8,0},{16,24},{24,16},{1,9},{9,1},{17,25},{25,17},{2,10},{10... | collective-permute-start | bytes 3145736 | tf_op jit(solution)/shard_map/ppermute | solution.py:183
  669.0 42.5 %collective-permute-start.68 = (bf16[2,64,2048]{2,1,0:T(8,128)(2,1)S(1)}, bf16[2,64,2048]{2,1,0:T(8,128)(2,1)S(1)}, u32[]{:S(2)}, u32[]{:S(2)}) collective-permute-start(bf16[2,64,2048]{2,1,0:T(8,128)(2,1)S(1)} %fusion.38), channel_id=1, source_target_pairs={{0,8},{8,0},{16,24},{24,16},{1,9},{9,1},{17,25},{25,17},{2,10},{10... | collective-permute-start | bytes 1572872 | tf_op jit(solution)/shard_map/ppermute | solution.py:183
  675.3 64.3 %collective-permute-start.35 = (bf16[1024,1024]{0,1:T(8,128)(2,1)}, bf16[1024,1024]{0,1:T(8,128)(2,1)}, u32[]{:S(2)}, u32[]{:S(2)}) collective-permute-start(bf16[1024,1024]{0,1:T(8,128)(2,1)} %convolution_convert_fusion.4), channel_id=1, source_target_pairs={{0,1},{1,0},{2,3},{3,2},{4,5},{5,4},{6,7},{7,6},{8,9},{9,8},{10,11... | collective-permute-start | bytes 6291464 | tf_op jit(solution)/shard_map/ppermute | solution.py:172
  725.2 71.7 %collective-permute-start.77 = (bf16[2048,512]{1,0:T(8,128)(2,1)}, bf16[2048,512]{1,0:T(8,128)(2,1)S(1)}, u32[]{:S(2)}, u32[]{:S(2)}) collective-permute-start(bf16[2048,512]{1,0:T(8,128)(2,1)} %get-tuple-element.92), channel_id=1, source_target_pairs={{0,1},{1,0},{2,3},{3,2},{4,5},{5,4},{6,7},{7,6},{8,9},{9,8},{10,11... | collective-permute-start | bytes 6291464 | tf_op jit(solution)/shard_map/ppermute | solution.py:172
  736.1 72.1 %collective-permute-start.72 = (bf16[64,2048]{1,0:T(8,128)(2,1)S(1)}, bf16[64,2048]{1,0:T(8,128)(2,1)}, u32[]{:S(2)}, u32[]{:S(2)}) collective-permute-start(bf16[64,2048]{1,0:T(8,128)(2,1)S(1)} %fusion.56), channel_id=1, source_target_pairs={{0,8},{8,0},{16,24},{24,16},{1,9},{9,1},{17,25},{25,17},{2,10},{10... | collective-permute-start | bytes 786440 | tf_op jit(solution)/shard_map/ppermute | solution.py:183
  736.7 73.1 %collective-permute-start.73 = (bf16[64,2048]{1,0:T(8,128)(2,1)S(1)}, bf16[64,2048]{1,0:T(8,128)(2,1)}, u32[]{:S(2)}, u32[]{:S(2)}) collective-permute-start(bf16[64,2048]{1,0:T(8,128)(2,1)S(1)} %fusion.56), channel_id=1, source_target_pairs={{0,16},{8,24},{16,0},{24,8},{1,17},{9,25},{17,1},{25,9},{2,18},{10... | collective-permute-start | bytes 786440 | tf_op jit(solution)/shard_map/ppermute | solution.py:183
  737.2 74.0 %collective-permute-start.74 = (bf16[64,2048]{1,0:T(8,128)(2,1)S(1)}, bf16[64,2048]{1,0:T(8,128)(2,1)}, u32[]{:S(2)}, u32[]{:S(2)}) collective-permute-start(bf16[64,2048]{1,0:T(8,128)(2,1)S(1)} %fusion.56), channel_id=1, source_target_pairs={{0,24},{8,16},{16,8},{24,0},{1,25},{9,17},{17,9},{25,1},{2,26},{10... | collective-permute-start | bytes 786440 | tf_op jit(solution)/shard_map/ppermute | solution.py:183
  799.4 76.9 %collective-permute-start.78 = (bf16[2,2,256,512]{3,2,0,1:T(8,128)(2,1)}, bf16[2,2,256,512]{3,2,0,1:T(8,128)(2,1)}, u32[]{:S(2)}, u32[]{:S(2)}) collective-permute-start(bf16[2,2,256,512]{3,2,0,1:T(8,128)(2,1)} %copy_bitcast_fusion), channel_id=1, source_target_pairs={{0,16},{8,24},{16,0},{24,8},{1,17},{9,25},{17,1},{25,9},{2,18},{10... | collective-permute-start | bytes 3145736 | tf_op jit(solution)/shard_map/ppermute | solution.py:183
  800.0 33.9 %collective-permute-start.61 = (f32[40,128]{1,0:T(8,128)S(1)}, f32[40,128]{1,0:T(8,128)S(1)}, u32[]{:S(2)}, u32[]{:S(2)}) collective-permute-start(f32[40,128]{1,0:T(8,128)S(1)} %maximum_bitcast_fusion), channel_id=1, source_target_pairs={{0,8},{8,0},{16,24},{24,16},{1,9},{9,1},{17,25},{25,17},{2,10},{10... | collective-permute-start | bytes 61448 | tf_op jit(solution)/shard_map/ppermute | solution.py:183
  808.2 29.6 %collective-permute-start.53 = (bf16[2,2,64,512]{3,2,0,1:T(8,128)(2,1)S(1)}, bf16[2,2,64,512]{3,2,0,1:T(8,128)(2,1)S(1)}, u32[]{:S(2)}, u32[]{:S(2)}) collective-permute-start(bf16[2,2,64,512]{3,2,0,1:T(8,128)(2,1)S(1)} %copy_bitcast_fusion.6), channel_id=1, source_target_pairs={{0,16},{8,24},{16,0},{24,8},{1,17},{9,25},{17,1},{25,9},{2,18},{10... | collective-permute-start | bytes 786440 | tf_op jit(solution)/shard_map/ppermute | solution.py:183
  809.7 32.5 %collective-permute-start.51 = (bf16[2,2,64,512]{3,2,0,1:T(8,128)(2,1)S(1)}, bf16[2,2,64,512]{3,2,0,1:T(8,128)(2,1)S(1)}, u32[]{:S(2)}, u32[]{:S(2)}) collective-permute-start(bf16[2,2,64,512]{3,2,0,1:T(8,128)(2,1)S(1)} %copy_bitcast_fusion.7), channel_id=1, source_target_pairs={{0,8},{8,0},{16,24},{24,16},{1,9},{9,1},{17,25},{25,17},{2,10},{10... | collective-permute-start | bytes 786440 | tf_op jit(solution)/shard_map/ppermute | solution.py:183
  (131 other events, 2404.8 us)

commit v3 on v2

--- a/solution.py
+++ b/solution.py
@@ -87,13 +87,13 @@
         dv_ref[...] = dv_acc[...].astype(jnp.bfloat16)
 
 
-def attention_specs(count, pairs, block):
+def attention_specs(count, pairs, block, skip=0):
     seg_col = pl.BlockSpec((count, 1), lambda h, i: (0, 0))
     seg_row = pl.BlockSpec((1, block), lambda h, i: (0, i))
-    query = pl.BlockSpec((block, PAIR), lambda h, i: (i, h))
-    key = pl.BlockSpec((count, PAIR), lambda h, i: (0, pairs + h))
-    value = pl.BlockSpec((count, PAIR), lambda h, i: (0, 2 * pairs + h))
-    lse = pl.BlockSpec((1, 2, block), lambda h, i: (h, 0, i))
+    query = pl.BlockSpec((block, PAIR), lambda h, i: (i, skip + h))
+    key = pl.BlockSpec((count, PAIR), lambda h, i: (0, pairs + skip + h))
+    value = pl.BlockSpec((count, PAIR), lambda h, i: (0, 2 * pairs + skip + h))
+    lse = pl.BlockSpec((1, 2, block), lambda h, i: (skip + h, 0, i))
     return seg_col, seg_row, query, key, value, lse
 
 
@@ -121,18 +121,20 @@
     )(segment.reshape(-1, 1), segment, qkv, qkv, qkv)
 
 
-def attend_back(qkv, segment, lse_rows, d_context):
+def attend_back(qkv, segment, lse_rows, d_context, turn, turns):
     count = qkv.shape[0]
     pairs = qkv.shape[1] // (3 * PAIR)
+    here = pairs // turns
     block = min(Q_BLOCK, count)
-    seg_col, seg_row, query, key, value, lse = attention_specs(count, pairs, block)
-    whole = pl.BlockSpec((count, PAIR), lambda h, i: (0, h))
-    shape = jax.ShapeDtypeStruct((count, pairs * PAIR), jnp.bfloat16)
+    seg_col, seg_row, query, key, value, lse = attention_specs(count, pairs, block, turn * here)
+    d_query = pl.BlockSpec((block, PAIR), lambda h, i: (i, h))
+    d_whole = pl.BlockSpec((count, PAIR), lambda h, i: (0, h))
+    shape = jax.ShapeDtypeStruct((count, here * PAIR), jnp.bfloat16)
     return pl.pallas_call(
         attend_back_kernel,
-        grid=(pairs, count // block),
+        grid=(here, count // block),
         in_specs=[seg_col, seg_row, query, key, value, lse, query],
-        out_specs=[query, whole, whole],
+        out_specs=[d_query, d_whole, d_whole],
         out_shape=[shape, shape, shape],
         scratch_shapes=[
             pltpu.VMEM((PAIR, count), jnp.bfloat16),
@@ -141,9 +143,9 @@
         ],
         compiler_params=pltpu.CompilerParams(vmem_limit_bytes=32 << 20),
         cost_estimate=pl.CostEstimate(
-            flops=40 * count * count * PAIR * pairs,
-            bytes_accessed=20 * count * pairs * PAIR,
-            transcendentals=2 * count * count * pairs,
+            flops=40 * count * count * PAIR * here,
+            bytes_accessed=20 * count * here * PAIR,
+            transcendentals=2 * count * count * here,
         ),
     )(segment.reshape(-1, 1), segment, qkv, qkv, qkv, lse_rows, d_context)
 
@@ -196,85 +198,106 @@
     return lax.axis_size("row") == 4 and lax.axis_size("dp") == 4 and rows % 128 == 0
 
 
-def place_kernel(idx, own, s1, s2, s3, near_x, near_y, far_a, far_b, out, sems):
-    quarter = s1.shape[0]
-    rows = own.shape[0]
+def place_kernel(idx, own, ring, near_x, near_y, far_a, far_b, *outs):
+    step = pl.program_id(0)
+    quarter = ring.shape[0]
     part = quarter // 2
-
-    def at(step, corner, skip, size):
-        start = idx[step] * rows + idx[4 + corner] * quarter + skip
-        return out.at[pl.ds(pl.multiple_of(start, part), size), :]
-
-    moves = [(own, out.at[pl.ds(pl.multiple_of(idx[0] * rows, rows), rows), :])]
-    for step, ref in ((1, s1), (2, s2), (3, s3)):
-        piece = pl.ds((step - 1) * quarter, quarter)
-        moves.append((ref, at(step, 0, 0, quarter)))
-        moves.append((near_x.at[piece, :], at(step, 1, 0, quarter)))
-        moves.append((near_y.at[piece, :], at(step, 2, 0, quarter)))
-    moves.append((far_a.at[pl.ds(0, quarter), :], at(1, 3, 0, quarter)))
-    moves.append((far_a.at[pl.ds(quarter, part), :], at(2, 3, 0, part)))
-    moves.append((far_b.at[pl.ds(0, part), :], at(2, 3, part, part)))
-    moves.append((far_b.at[pl.ds(part, quarter), :], at(3, 3, 0, quarter)))
-    copies = [
-        pltpu.make_async_copy(source, target, sems.at[i])
-        for i, (source, target) in enumerate(moves)
-    ]
-    for copy in copies:
-        copy.start()
-    for copy in copies:
-        copy.wait()
-
-
-def place(idx, own, *pieces):
+    begin = 0
+    for out in outs:
+        columns = slice(begin, begin + out.shape[1])
+        begin = begin + out.shape[1]
+
+        def put(corner, skip, value):
+            start = pl.multiple_of(idx[4 + corner] * quarter + skip, part)
+            out[pl.ds(start, value.shape[0]), :] = value
+
+        @pl.when(step == 0)
+        def _():
+            out[...] = own[:, columns]
+
+        @pl.when(step > 0)
+        def _():
+            put(0, 0, ring[:, columns])
+            put(1, 0, near_x[:, columns])
+            put(2, 0, near_y[:, columns])
+
+        @pl.when(step == 1)
+        def _():
+            put(3, 0, far_a[:quarter, columns])
+
+        @pl.when(step == 2)
+        def _():
+            put(3, 0, far_a[quarter:, columns])
+            put(3, part, far_b[:part, columns])
+
+        @pl.when(step == 3)
+        def _():
+            put(3, 0, far_b[part:, columns])
+
+
+def place(idx, own, ring, near_x, near_y, far_a, far_b, widths):
     rows, width = own.shape
+    fixed = [pl.BlockSpec(part.shape, lambda s, idx: (0, 0)) for part in (own, far_a, far_b)]
+    moving = pl.BlockSpec((rows // 4, width), lambda s, idx: (jnp.maximum(s - 1, 0), 0))
     return pl.pallas_call(
         place_kernel,
-        in_specs=[pl.BlockSpec(memory_space=pltpu.SMEM)]
-        + [pl.BlockSpec(memory_space=pl.ANY)] * 8,
-        out_specs=pl.BlockSpec(memory_space=pl.ANY),
-        out_shape=jax.ShapeDtypeStruct((4 * rows, width), own.dtype),
-        scratch_shapes=[pltpu.SemaphoreType.DMA((14,))],
+        grid_spec=pltpu.PrefetchScalarGridSpec(
+            num_scalar_prefetch=1,
+            grid=(4,),
+            in_specs=[fixed[0], moving, moving, moving, fixed[1], fixed[2]],
+            out_specs=[pl.BlockSpec((rows, w), lambda s, idx: (idx[s], 0)) for w in widths],
+        ),
+        out_shape=[jax.ShapeDtypeStruct((4 * rows, w), own.dtype) for w in widths],
+        compiler_params=pltpu.CompilerParams(vmem_limit_bytes=40 << 20),
         cost_estimate=pl.CostEstimate(
             flops=0, bytes_accessed=8 * rows * width * 2, transcendentals=0
         ),
-    )(idx, own, *pieces)
-
-
-def whole_weights(blocks):
+    )(idx, own, ring, near_x, near_y, far_a, far_b)
+
+
+def natural_order(whole):
+    cut = whole.shape[0] // 2
+    return jnp.where(
+        lax.axis_index("col") == 0, whole, jnp.concatenate([whole[cut:], whole[:cut]], axis=0)
+    )
+
+
+def gathered(block):
+    rows = block.shape[0] // lax.axis_size("dp")
+    part = lax.dynamic_slice_in_dim(block, lax.axis_index("dp") * rows, rows, 0)
+    return natural_order(lax.all_gather(part, ("row", "dp"), axis=0, tiled=True))
+
+
+def whole_weights(groups):
     core, corner = lax.axis_index("col"), lax.axis_index("dp")
     size = lax.axis_size("row")
-    if not all(is_small_grid(block.shape[0]) for block in blocks):
-        wholes = []
-        for block in blocks:
-            rows = block.shape[0] // lax.axis_size("dp")
-            part = lax.dynamic_slice_in_dim(block, corner * rows, rows, 0)
-            full = lax.all_gather(part, ("row", "dp"), axis=0, tiled=True)
-            cut = full.shape[0] // 2
-            wholes.append(
-                jnp.where(core == 0, full, jnp.concatenate([full[cut:], full[:cut]], axis=0))
-            )
-        return wholes
+    if not all(is_small_grid(block.shape[0]) for group in groups for block in group):
+        return [[gathered(block) for block in group] for group in groups]
     place_z = (lax.axis_index("row") + size // 2 * core + size - jnp.arange(size)) % size
     idx = jnp.concatenate([place_z, corner ^ jnp.arange(4)]).astype(jnp.int32)
+    owns = [jnp.concatenate(group, axis=1) if len(group) > 1 else group[0] for group in groups]
+    stacks = []
+    for own in owns:
+        quarter = own.shape[0] // 4
+        part = lax.dynamic_slice_in_dim(own, corner * quarter, quarter, 0)
+        if stacks:
+            part = after(part, stacks[-1])
+        stacks.append(
+            jnp.concatenate([shifted(part, step) for step in (1, 2, 3)], axis=0)
+        )
     wholes = []
-    earlier_z = earlier_xy = None
-    for block in blocks:
-        quarter = block.shape[0] // 4
-        part = lax.dynamic_slice_in_dim(block, corner * quarter, quarter, 0)
-        if earlier_z is not None:
-            part = after(part, earlier_z)
-        ring = [shifted(part, step) for step in (1, 2, 3)]
-        earlier_z = ring[0]
-        stack = jnp.concatenate(ring, axis=0)
-        if earlier_xy is not None:
-            stack = after(stack, earlier_xy)
+    earlier = None
+    for own, stack, group in zip(owns, stacks, groups):
+        if earlier is not None:
+            stack = after(stack, earlier)
         near_x = partner(stack, "dp", 1)
         near_y = partner(stack, "dp", 2)
         cut = stack.shape[0] // 2
         far_a = partner(near_y[:cut], "dp", 1)
         far_b = partner(near_x[cut:], "dp", 2)
-        earlier_xy = near_x
-        wholes.append(place(idx, block, *ring, near_x, near_y, far_a, far_b))
+        earlier = (far_a, far_b)
+        widths = [block.shape[1] for block in group]
+        wholes.append(place(idx, own, stack, near_x, near_y, far_a, far_b, widths))
     return wholes
 
 
@@ -289,46 +312,88 @@
     return total.astype(jnp.bfloat16)
 
 
-def reduced_weight(grad):
-    core, corner, level = lax.axis_index("col"), lax.axis_index("dp"), lax.axis_index("row")
-    size = lax.axis_size("row")
-    if not is_small_grid(grad.shape[0] // size):
-        cut = grad.shape[0] // 2
-        grad = jnp.where(core == 0, grad, jnp.concatenate([grad[cut:], grad[:cut]], axis=0))
-        part = lax.psum_scatter(grad, ("row", "dp"), scatter_dimension=0, tiled=True)
-        return lax.all_gather(part, "dp", axis=0, tiled=True).astype(jnp.float32)
-    a, b = corner // 2, corner % 2
-    width = grad.shape[1]
-    six = grad.reshape(2, 2, 2, 2, -1, width)
-    first, second = six[0], six[1]
-    got_first = partner(pick(first, 2, 1 - b), "dp", 1)
-    got_second = partner(pick(second, 1, 1 - a), "dp", 2)
-    send_first = added(pick(pick(first, 2, b), 1, 1 - a), pick(got_first, 1, 1 - a))
-    send_second = added(pick(pick(second, 1, a), 1, 1 - b), pick(got_second, 1, 1 - b))
-    far_first = partner(send_first, "dp", 2)
-    far_second = partner(send_second, "dp", 1)
-    keep_first = added(pick(pick(first, 2, b), 1, a), pick(got_first, 1, a), far_first)
-    keep_second = added(pick(pick(second, 1, a), 1, b), pick(got_second, 1, b), far_second)
-    levels = jnp.concatenate([keep_first, keep_second], axis=0)
-
-    def of_level(index):
-        return pick(levels, 0, (index + size // 2 * core) % size)
-
-    total = added(
-        of_level(level), *[shifted(of_level((level + step) % size), step) for step in (1, 2, 3)]
-    )
-    others = [total] + [partner(total, "dp", bit) for bit in (1, 2, 3)]
-    return jnp.concatenate(
-        [
-            jnp.where(
-                a == 0,
-                jnp.where(b == 0, others[k], others[k ^ 1]),
-                jnp.where(b == 0, others[k ^ 2], others[k ^ 3]),
+class Reduction:
+    def __init__(self, first, second):
+        corner = lax.axis_index("dp")
+        self.a, self.b = corner // 2, corner % 2
+        self.direct = not is_small_grid(2 * first.shape[0] // lax.axis_size("row"))
+        self.step = 0
+        if self.direct:
+            self.whole = jnp.concatenate([first, second], axis=0)
+        else:
+            width = first.shape[1]
+            self.first = first.reshape(2, 2, 2, -1, width)
+            self.second = second.reshape(2, 2, 2, -1, width)
+
+    def sends(self):
+        if self.direct:
+            return []
+        a, b = self.a, self.b
+        if self.step == 0:
+            return [pick(self.first, 2, 1 - b), pick(self.second, 1, 1 - a)]
+        if self.step == 1:
+            one, two = self.got
+            self.keep = (
+                pick(pick(self.first, 2, b), 1, a),
+                pick(one, 1, a),
+                pick(pick(self.second, 1, a), 1, b),
+                pick(two, 1, b),
             )
-            for k in range(4)
-        ],
-        axis=0,
-    ).astype(jnp.float32)
+            return [
+                added(pick(pick(self.first, 2, b), 1, 1 - a), pick(one, 1, 1 - a)),
+                added(pick(pick(self.second, 1, a), 1, 1 - b), pick(two, 1, 1 - b)),
+            ]
+        if self.step == 2:
+            levels = jnp.concatenate(
+                [added(*self.keep[:2], self.got[0]), added(*self.keep[2:], self.got[1])], axis=0
+            )
+            size = lax.axis_size("row")
+            place_z = lax.axis_index("row") + size // 2 * lax.axis_index("col")
+            parts = [pick(levels, 0, (place_z + step) % size) for step in range(4)]
+            self.mine = parts[0]
+            return parts[1:]
+        self.total = added(self.mine, *self.got)
+        return [self.total]
+
+    def go(self, sends):
+        if self.direct:
+            return
+        if self.step == 0:
+            self.got = [partner(sends[0], "dp", 1), partner(sends[1], "dp", 2)]
+        elif self.step == 1:
+            self.got = [partner(sends[0], "dp", 2), partner(sends[1], "dp", 1)]
+        elif self.step == 2:
+            self.got = [shifted(part, step) for part, step in zip(sends, (1, 2, 3))]
+        else:
+            self.got = [sends[0]] + [partner(sends[0], "dp", bit) for bit in (1, 2, 3)]
+        self.step = self.step + 1
+
+    def advance(self, values=None):
+        sends = self.sends()
+        if values is not None:
+            values, *sends = lax.optimization_barrier((values, *sends))
+        self.go(sends)
+        return values
+
+    def result(self):
+        if self.direct:
+            whole = natural_order(self.whole)
+            part = lax.psum_scatter(whole, ("row", "dp"), scatter_dimension=0, tiled=True)
+            return lax.all_gather(part, "dp", axis=0, tiled=True).astype(jnp.float32)
+        while self.step < 4:
+            self.advance()
+        got = self.got
+        return jnp.concatenate(
+            [
+                jnp.where(
+                    self.a == 0,
+                    jnp.where(self.b == 0, got[k], got[k ^ 1]),
+                    jnp.where(self.b == 0, got[k ^ 2], got[k ^ 3]),
+                )
+                for k in range(4)
+            ],
+            axis=0,
+        ).astype(jnp.float32)
 
 
 def reduced_vector(values):
@@ -379,8 +444,8 @@
 ):
     half = w_query.shape[1]
     token_rows = jnp.concatenate([tokens, swapped(tokens)], axis=1)
-    w_qkv, wo_half, wu, wd_half = whole_weights(
-        [jnp.concatenate([w_query, w_key, w_value], axis=1), w_out, w_up, w_down]
+    (w_qkv,), (wo_half, wu), (wd_half,) = whole_weights(
+        [[jnp.concatenate([w_query, w_key, w_value], axis=1)], [w_out, w_up], [w_down]]
     )
     cotangent_rows = jnp.concatenate([cotangent, swapped(cotangent)], axis=1)
     own_vectors = jnp.stack([b_out, b_down, gain_one, shift_one, gain_two, shift_two])
@@ -414,36 +479,52 @@
     d_gain_two = jnp.sum(y * normed_two, axis=0)
     d_shift_two = jnp.sum(y, axis=0)
     ffn_grad = second_grad.astype(jnp.bfloat16)
-    d_w_down = matmul_tn(activated, ffn_grad).astype(jnp.bfloat16)
-    o_w_down = reduced_weight(
-        jnp.concatenate([d_w_down[:, :half], swapped(d_w_down[:, half:])], axis=0)
-    )
+    d_down_other = swapped(matmul_tn(activated, ffn_grad[:, half:]).astype(jnp.bfloat16))
+    d_down_own = matmul_tn(activated, ffn_grad[:, :half]).astype(jnp.bfloat16)
     d_b_down = column_sum(ffn_grad)
     pre_grad = (matmul_nt(ffn_grad, wd) * slope).astype(jnp.bfloat16)
-    o_w_up = reduced_weight(matmul_tn(hidden, pre_grad).astype(jnp.bfloat16))
     d_b_up = column_sum(pre_grad)
+    down = Reduction(d_down_own, d_down_other)
+    pre_grad = down.advance(pre_grad)
     hidden_part = matmul_nt(pre_grad, wu).astype(jnp.bfloat16)
-    hidden_grad = second_grad + (
-        hidden_part.astype(jnp.float32) + swapped_rows(hidden_part)
-    )
+    hidden_other = swapped_rows(hidden_part)
+    d_w_up = matmul_tn(hidden, pre_grad).astype(jnp.bfloat16)
+    up = Reduction(d_w_up[:half], d_w_up[half:])
+    hidden_part = up.advance(hidden_part)
+    hidden_grad = second_grad + (hidden_part.astype(jnp.float32) + hidden_other)
     first_grad = norm_backward(hidden_grad, normed_one, inverse_one, gain1)
     d_gain_one = jnp.sum(hidden_grad * normed_one, axis=0)
     d_shift_one = jnp.sum(hidden_grad, axis=0)
     branch_grad = first_grad.astype(jnp.bfloat16)
-    o_w_out = reduced_weight(matmul_tn(context_rows, branch_grad[:, :half]).astype(jnp.bfloat16))
+    branch_grad = down.advance(branch_grad)
     d_b_out = column_sum(branch_grad)
     wide = jnp.stack([d_b_out, d_b_down, d_gain_one, d_shift_one, d_gain_two, d_shift_two])
+    context_grad = matmul_nt(branch_grad, wo[:half]).astype(jnp.bfloat16)
+    d_w_out = matmul_tn(context_rows, branch_grad[:, :half]).astype(jnp.bfloat16)
+    out = Reduction(d_w_out[:half], d_w_out[half:])
+    context_grad = out.advance(context_grad)
+    grads = list(attend_back(qkv, segment, lse_rows, context_grad, 0, 2))
+    grads[0] = up.advance(grads[0])
+    context_grad = down.advance(lax.optimization_barrier((context_grad, *grads))[0])
+    grads_more = attend_back(qkv, segment, lse_rows, context_grad, 1, 2)
+    qkv_grad = jnp.concatenate(
+        [part for pair in zip(grads, grads_more) for part in pair], axis=1
+    )
+    qkv_grad = up.advance(qkv_grad)
+    qkv_grad = out.advance(qkv_grad)
+    d_w_qkv = matmul_tn(token_rows, qkv_grad).astype(jnp.bfloat16)
+    w_qkv_grad = Reduction(d_w_qkv[:half], d_w_qkv[half:])
+    qkv_grad = w_qkv_grad.advance(qkv_grad)
+    token_part = matmul_nt(qkv_grad, w_qkv).astype(jnp.bfloat16)
+    token_other = swapped(token_part[:, half:])
+    token_part = down.advance(token_part)
+    d_b_qkv = column_sum(qkv_grad)
+    token_sum = token_part[:, :half].astype(jnp.float32) + token_other.astype(jnp.float32)
+    d_tokens = (token_sum + first_grad[:, :half]).astype(jnp.bfloat16)
     sums = reduced_vector(jnp.concatenate([wide[:, :half].reshape(-1), d_b_up]))
-    context_grad = matmul_nt(branch_grad, wo[:half]).astype(jnp.bfloat16)
-    qkv_grad = jnp.concatenate(attend_back(qkv, segment, lse_rows, context_grad), axis=1)
-    o_w_qkv = reduced_weight(matmul_tn(token_rows, qkv_grad).astype(jnp.bfloat16))
-    d_b_qkv = column_sum(qkv_grad)
     d_b_qv = reduced_vector(jnp.concatenate([d_b_qkv[:half], d_b_qkv[2 * half :]]))
-    token_part = matmul_nt(qkv_grad, w_qkv).astype(jnp.bfloat16)
-    token_sum = token_part[:, :half].astype(jnp.float32) + swapped(
-        token_part[:, half:]
-    ).astype(jnp.float32)
-    d_tokens = (token_sum + first_grad[:, :half]).astype(jnp.bfloat16)
+    o_w_down, o_w_up, o_w_out = down.result(), up.result(), out.result()
+    o_w_qkv = w_qkv_grad.result()
     pieces = [sums[i * half : (i + 1) * half] for i in range(6)]
     return (
         output,

time: 951 us -> 553 us (0.58)
  Pallas kernels: 452 us -> 69.6 us
  matrix products: 78 us -> 64.8 us
    pallas_call x5, Pallas kernels: 424 us -> 41.5 us  [the longest x2 35.2 us: attend_back(): pl.pallas_call(attend_back_kernel, grid=(here, count // block), in_specs=...]
    ppermute x52 -> x48, waiting for transfers between devices: 156 us -> 136 us  [partner(): return lax.ppermute(part, axis, [(i, i ^ bit) for i in range(size)])]
    ppermute x24 -> x21, waiting for transfers between devices: 55.7 us -> 68 us  [shifted(): lax.ppermute(part, 'row', [(i, (i + step) % size) for i in range(size)])]
    dot_general x4, matrix products: 36.1 us -> 24.9 us  [matmul(): return jnp.dot(left, right, preferred_element_type=jnp.float32)]
    convert_element_type x20, other arithmetic: 9.75 us -> 20.3 us  [added(): return total.astype(jnp.bfloat16)]
    ppermute x24 -> x21, starting transfers between devices: 47.6 us -> 39.9 us  [shifted(): lax.ppermute(part, 'row', [(i, (i + step) % size) for i in range(size)])]
    dot_general x4 -> x5, matrix products: 21 us -> 16.2 us  [matmul_tn(): lax.dot_general(left, right, (((0,), (0,)), ((), ())), preferred_element_...]
    ppermute x52 -> x48, starting transfers between devices: 54.7 us -> 59.3 us  [partner(): return lax.ppermute(part, axis, [(i, i ^ bit) for i in range(size)])]
  transfers between devices with their start and end apart: 86 -> 79, of which waited for: 34 -> 32; matrix products, arithmetic and copies ran while one was open for 13% -> 20% of each run, Pallas kernels for 48% -> 13%
where the time goes in v3:
time: 553 us; the launch traced here: 546 us
  waiting for transfers between devices  207 us (37%)
  starting transfers between devices  101 us (18%)
  Pallas kernels  69.6 us (13%)
  matrix products  64.8 us (12%)
  other arithmetic  54.9 us (10%)
  local copies, waits for them, and re-layouts  46.6 us (8%)
    ppermute x48, waiting for transfers between devices, partner(): return lax.ppermute(part, axis, [(i, i ^ bit) for i in range(size)])  136 us
    ppermute x21, waiting for transfers between devices, shifted(): lax.ppermute(part, 'row', [(i, (i + step) % size) for i in range(size)])  68 us
    ppermute x48, starting transfers between devices, partner(): return lax.ppermute(part, axis, [(i, i ^ bit) for i in range(size)])  59.3 us
    ppermute x21, starting transfers between devices, shifted(): lax.ppermute(part, 'row', [(i, (i + step) % size) for i in range(size)])  39.9 us
    pallas_call x2, Pallas kernels, attend_back(): pl.pallas_call(attend_back_kernel, grid=(here, count // block), in_specs=...  35.2 us
    pallas_call x1, Pallas kernels, attend(): pl.pallas_call(attend_kernel, grid=(pairs, count // block), in_specs=[seg...  28.2 us
    dot_general x4, matrix products, matmul(): return jnp.dot(left, right, preferred_element_type=jnp.float32)  24.9 us
    dot_general x4, matrix products, matmul_nt(): lax.dot_general(left, right, (((1,), (1,)), ((), ())), preferred_element_...  23.7 us
  transfers between devices with their start and end apart: 79, of which 32 were waited for; matrix products, arithmetic and copies ran while one was open for 20% of the time, Pallas kernels for 13%

profile of v3, /device:TPU:0, one launch (start us, length us, event | category | flops | bytes accessed | tf_op | source)
XLA Modules:
  0.0 545.8 jit_solution(13717729709777759033)
XLA Ops:
  15.3 6.9 %collective-permute-done.2 = bf16[64,1536]{1,0:T(8,128)(2,1)S(1)} collective-permute-done((bf16[64,1536]{1,0:T(8,128)(2,1)S(1)}, bf16[64,1536]{1,0:T(8,128)(2,1)S(1)}, u32[]{:S(2)}, u32[]{:S(2)}) %collective-permute-start.2) | collective-permute-done | bytes 196640 | tf_op jit(solution)/shard_map/ppermute | solution.py:190
  40.7 9.8 %collective-permute-done.10 = bf16[64,2560]{1,0:T(8,128)(2,1)S(1)} collective-permute-done((bf16[64,2560]{1,0:T(8,128)(2,1)}, bf16[64,2560]{1,0:T(8,128)(2,1)S(1)}, u32[]{:S(2)}, u32[]{:S(2)}) %collective-permute-start.10) | collective-permute-done | bytes 327712 | tf_op jit(solution)/shard_map/ppermute | solution.py:190
  53.8 5.8 %collective-permute-done.6.far_a = bf16[96,1536]{1,0:T(8,128)(2,1)S(1)} collective-permute-done((bf16[96,1536]{1,0:T(8,128)(2,1)S(1)}, bf16[96,1536]{1,0:T(8,128)(2,1)S(1)}, u32[]{:S(2)}, u32[]{:S(2)}) %collective-permute-start.6) | collective-permute-done | bytes 294944 | tf_op jit(solution)/shard_map/ppermute | solution.py:185
  63.0 8.1 %collective-permute-start.20 = (bf16[256,512]{1,0:T(8,128)(2,1)S(1)}, bf16[256,512]{1,0:T(8,128)(2,1)S(1)}, u32[]{:S(2)}, u32[]{:S(2)}) collective-permute-start(bf16[256,512]{1,0:T(8,128)(2,1)S(1)} %constant_dynamic-slice_fusion.8), channel_id=1, source_target_pairs={{0,6},{2,0},{4,2},{6,4},{1,7},{3,1},{5,3},{7,5},{8,14},{10,8},{12,... | collective-permute-start | bytes 786440 | tf_op jit(solution)/shard_map/ppermute | solution.py:190
  86.9 28.2 %shard_map.306 = (bf16[1024,512]{1,0:T(8,128)(2,1)}, f32[4,2,1024]{2,1,0:T(2,128)S(1)}) custom-call(s32[1024,1]{1,0:T(8,128)S(1)} %copy-done.3, s32[1,1024]{1,0:T(1,128)S(1)} %copy-done.5, bf16[1024,1536]{1,0:T(8,128)(2,1)S(1)} %add_convert_fusion.q_ref.k_ref.v_ref, bf16[1024,1536]{1,0:T(8,128)(2,1)S(1)} %add_convert_fusion.q_ref.k_ref.v_ref, ...), custom_call_target="tpu_custom_call" | custom-call | flops 8589934592 | bytes 5242880 | tf_op jit(solution)/shard_map/pallas_call | solution.py:105
  124.0 15.7 %collective-permute-done.22.near_y = bf16[768,512]{1,0:T(8,128)(2,1)S(1)} collective-permute-done((bf16[768,512]{1,0:T(8,128)(2,1)S(1)}, bf16[768,512]{1,0:T(8,128)(2,1)S(1)}, u32[]{:S(2)}, u32[]{:S(2)}) %collective-permute-start.22) | collective-permute-done | bytes 786464 | tf_op jit(solution)/shard_map/ppermute | solution.py:185
  157.6 9.5 %multiply_convert_fusion = (bf16[1024,2048]{1,0:T(8,128)(2,1)S(1)}, f32[1024,2048]{1,0:T(8,128)}) fusion(f32[2048]{0:T(1024)S(1)} %convert_element_type.455, bf16[1024,2048]{1,0:T(8,128)(2,1)S(1)} %copy-done.7, f32[1024,1024]{0,1:T(8,128)S(1)} %get-tuple-element.226, f32[1024]{0:T(1024)S(1)} %bitcast.286, f32[1024]{0:T(1024)S(1)} %bitcast.276, ...), kind=kOutput, calls=%fused_computation.8 | convolution fusion | flops 4312793088 | bytes 20996096 | tf_op jit(solution)/shard_map/dot_general | solution.py:154
  197.7 9.6 %convert_reduce_fusion = (f32[2048]{0:T(1024)S(1)}, bf16[1024,2048]{1,0:T(8,128)(2,1)S(1)}) fusion(f32[1024,2048]{1,0:T(8,128)} %get-tuple-element.228, f32[2048]{0:T(1024)S(1)} %convert_element_type.455, bf16[1024,1024]{0,1:T(8,128)(2,1)S(1)} %get-tuple-element.156, bf16[2048,512]{1,0:T(8,128)(2,1)S(1)} %copy-done.73, bf16[2048,512]{1,0:T(8,128)(2,1)S(1)} %copy-done.39), kind=kOutput, calls=%fused_computation.7 | convolution fusion | flops 4330616832 | bytes 18890752 | tf_op jit(solution)/shard_map/dot_general | solution.py:164
  208.5 5.9 %convolution_convert_fusion.5 = bf16[1024,1024]{0,1:T(8,128)(2,1)} fusion(bf16[1024,2048]{1,0:T(8,128)(2,1)S(1)} %get-tuple-element.71, bf16[1024,2048]{1,0:T(8,128)(2,1)S(1)} %copy-done.8), kind=kOutput, calls=%fused_computation.56 | convolution fusion | flops 4296015872 | bytes 10485760 | tf_op jit(solution)/shard_map/dot_general | solution.py:164
  229.0 18.8 %collective-permute-done.30 = bf16[2,2,256,512]{3,2,0,1:T(8,128)(2,1)} collective-permute-done((bf16[2,2,256,512]{3,2,0,1:T(8,128)(2,1)}, bf16[2,2,256,512]{3,2,0,1:T(8,128)(2,1)}, u32[]{:S(2)}, u32[]{:S(2)}) %collective-permute-start.30) | collective-permute-done | bytes 1048608 | tf_op jit(solution)/shard_map/ppermute | solution.py:185
  252.3 17.2 %collective-permute-done.32 = bf16[2,2,64,2048]{3,2,0,1:T(8,128)(2,1)} collective-permute-done((bf16[2,2,64,2048]{3,2,0,1:T(8,128)(2,1)}, bf16[2,2,64,2048]{3,2,0,1:T(8,128)(2,1)}, u32[]{:S(2)}, u32[]{:S(2)}) %collective-permute-start.32) | collective-permute-done | bytes 1048608 | tf_op jit(solution)/shard_map/ppermute | solution.py:185
  275.4 6.3 %multiply_reduce_fusion = (f32[1024]{0:T(1024)S(1)}, f32[1024]{0:T(1024)S(1)}, f32[1024]{0:T(1024)S(1)}, f32[1024]{0:T(1024)S(1)}, f32[1024,1024]{0,1:T(8,128)S(1)}) fusion(f32[1024,1024]{0,1:T(8,128)S(1)} %copy-done.13, f32[1024]{0:T(1024)S(1)} %get-tuple-element.225, f32[1024]{0:T(1024)S(1)} %get-tuple-element.224, f32[1024]{0:T(1024)S(1)} %bitcast.280, ...), kind=kLoop, calls=%fused_computation.23 | loop fusion | flops 26210304 | bytes 18919424 | tf_op jit(solution)/shard_map/reduce_sum | solution.py:496
  296.9 17.7 %shard_map.309 = (bf16[1024,256]{1,0:T(8,128)(2,1)S(1)}, bf16[1024,256]{1,0:T(8,128)(2,1)S(1)}, bf16[1024,256]{1,0:T(8,128)(2,1)S(1)}) custom-call(s32[1024,1]{1,0:T(8,128)S(1)} %copy-done.4, s32[1,1024]{1,0:T(1,128)S(1)} %copy-done.5, bf16[1024,1536]{1,0:T(8,128)(2,1)S(1)} %copy-done.10, bf16[1024,1536]{1,0:T(8,128)(2,1)S(1)} %copy-done.10, ...), custom_call_target="tpu_custom_call" | custom-call | flops 10737418240 | bytes 5242880 | tf_op jit(solution)/shard_map/pallas_call | solution.py:133
  326.9 6.4 %collective-permute-done.38 = bf16[2,2,64,512]{3,2,0,1:T(8,128)(2,1)S(1)} collective-permute-done((bf16[2,2,64,512]{3,2,0,1:T(8,128)(2,1)}, bf16[2,2,64,512]{3,2,0,1:T(8,128)(2,1)S(1)}, u32[]{:S(2)}, u32[]{:S(2)}) %collective-permute-start.38) | collective-permute-done | bytes 262176 | tf_op jit(solution)/shard_map/ppermute | solution.py:185
  340.4 17.5 %shard_map.310 = (bf16[1024,256]{1,0:T(8,128)(2,1)S(1)}, bf16[1024,256]{1,0:T(8,128)(2,1)S(1)}, bf16[1024,256]{1,0:T(8,128)(2,1)S(1)}) custom-call(s32[1024,1]{1,0:T(8,128)S(1)} %copy-done.4, s32[1,1024]{1,0:T(1,128)S(1)} %copy-done.5, bf16[1024,1536]{1,0:T(8,128)(2,1)S(1)} %copy-done.10, bf16[1024,1536]{1,0:T(8,128)(2,1)S(1)} %copy-done.10, ...), custom_call_target="tpu_custom_call" | custom-call | flops 10737418240 | bytes 5242880 | tf_op jit(solution)/shard_map/pallas_call | solution.py:133
  381.0 8.1 %collective-permute-start.56 = (f32[8,128]{1,0:T(8,128)S(1)}, f32[8,128]{1,0:T(8,128)S(1)}, u32[]{:S(2)}, u32[]{:S(2)}) collective-permute-start(f32[8,128]{1,0:T(8,128)S(1)} %add.569), channel_id=1, source_target_pairs={{0,2},{2,0},{4,6},{6,4},{1,3},{3,1},{5,7},{7,5},{8,10},{10,8},{12,... | collective-permute-start | bytes 12296 | tf_op jit(solution)/shard_map/ppermute | solution.py:185
  397.3 5.8 %convolution_convert_fusion.4 = bf16[1024,1024]{0,1:T(8,128)(2,1)S(1)} fusion(bf16[1024,1536]{1,0:T(8,128)(2,1)} %copy-done.33, bf16[1024,1536]{1,0:T(8,128)(2,1)S(1)} %copy-done.1), kind=kOutput, calls=%fused_computation.55 | convolution fusion | flops 3222274048 | bytes 8388608 | tf_op jit(solution)/shard_map/dot_general | solution.py:164
  410.5 15.9 %collective-permute-done.61 = bf16[64,512]{1,0:T(8,128)(2,1)S(1)} collective-permute-done((bf16[64,512]{1,0:T(8,128)(2,1)S(1)}, bf16[64,512]{1,0:T(8,128)(2,1)S(1)}, u32[]{:S(2)}, u32[]{:S(2)}) %collective-permute-start.61) | collective-permute-done | bytes 65568 | tf_op jit(solution)/shard_map/ppermute | solution.py:190
  431.0 5.9 %collective-permute-done.42 = bf16[256,512]{1,0:T(8,128)(2,1)S(1)} collective-permute-done((bf16[256,512]{1,0:T(8,128)(2,1)S(1)}, bf16[256,512]{1,0:T(8,128)(2,1)S(1)}, u32[]{:S(2)}, u32[]{:S(2)}) %collective-permute-start.42) | collective-permute-done | bytes 262176 | tf_op jit(solution)/shard_map/ppermute | solution.py:190
  437.4 12.8 %collective-permute-done.41 = bf16[256,512]{1,0:T(8,128)(2,1)S(1)} collective-permute-done((bf16[256,512]{1,0:T(8,128)(2,1)S(1)}, bf16[256,512]{1,0:T(8,128)(2,1)S(1)}, u32[]{:S(2)}, u32[]{:S(2)}) %collective-permute-start.41) | collective-permute-done | bytes 262176 | tf_op jit(solution)/shard_map/ppermute | solution.py:190
  472.4 15.7 %collective-permute-done.46 = bf16[2,2,64,1536]{3,2,0,1:T(8,128)(2,1)S(1)} collective-permute-done((bf16[2,2,64,1536]{3,2,0,1:T(8,128)(2,1)S(1)}, bf16[2,2,64,1536]{3,2,0,1:T(8,128)(2,1)S(1)}, u32[]{:S(2)}, u32[]{:S(2)}) %collective-permute-start.46) | collective-permute-done | bytes 786464 | tf_op jit(solution)/shard_map/ppermute | solution.py:185
  488.2 14.8 %collective-permute-done.45 = bf16[2,64,1536]{2,1,0:T(8,128)(2,1)S(1)} collective-permute-done((bf16[2,64,1536]{2,1,0:T(8,128)(2,1)S(1)}, bf16[2,64,1536]{2,1,0:T(8,128)(2,1)S(1)}, u32[]{:S(2)}, u32[]{:S(2)}) %collective-permute-start.45) | collective-permute-done | bytes 393248 | tf_op jit(solution)/shard_map/ppermute | solution.py:185
  504.0 8.1 %collective-permute-done.47 = bf16[2,64,1536]{2,1,0:T(8,128)(2,1)S(1)} collective-permute-done((bf16[2,64,1536]{2,1,0:T(8,128)(2,1)S(1)}, bf16[2,64,1536]{2,1,0:T(8,128)(2,1)S(1)}, u32[]{:S(2)}, u32[]{:S(2)}) %collective-permute-start.47) | collective-permute-done | bytes 393248 | tf_op jit(solution)/shard_map/ppermute | solution.py:185
  520.6 12.5 %collective-permute-done.49 = bf16[64,1536]{1,0:T(8,128)(2,1)S(1)} collective-permute-done((bf16[64,1536]{1,0:T(8,128)(2,1)S(1)}, bf16[64,1536]{1,0:T(8,128)(2,1)S(1)}, u32[]{:S(2)}, u32[]{:S(2)}) %collective-permute-start.49) | collective-permute-done | bytes 196640 | tf_op jit(solution)/shard_map/ppermute | solution.py:190
  (435 shorter events, 260.3 us)
Async XLA Ops:
  29.8 44.0 %collective-permute-start = (bf16[1024,512]{0,1:T(8,128)(2,1)}, bf16[1024,512]{0,1:T(8,128)(2,1)}, u32[]{:S(2)}, u32[]{:S(2)}) collective-permute-start(bf16[1024,512]{0,1:T(8,128)(2,1)} %copy.68), channel_id=1, source_target_pairs={{0,1},{1,0},{2,3},{3,2},{4,5},{5,4},{6,7},{7,6},{8,9},{9,8},{10,11... | collective-permute-start | bytes 3145736 | tf_op jit(solution)/shard_map/ppermute | solution.py:174
  63.0 57.0 %collective-permute-start.20 = (bf16[256,512]{1,0:T(8,128)(2,1)S(1)}, bf16[256,512]{1,0:T(8,128)(2,1)S(1)}, u32[]{:S(2)}, u32[]{:S(2)}) collective-permute-start(bf16[256,512]{1,0:T(8,128)(2,1)S(1)} %constant_dynamic-slice_fusion.8), channel_id=1, source_target_pairs={{0,6},{2,0},{4,2},{6,4},{1,7},{3,1},{5,3},{7,5},{8,14},{10,8},{12,... | collective-permute-start | bytes 786440 | tf_op jit(solution)/shard_map/ppermute | solution.py:190
  71.1 48.9 %collective-permute-start.19 = (bf16[256,512]{1,0:T(8,128)(2,1)S(1)}, bf16[256,512]{1,0:T(8,128)(2,1)S(1)}, u32[]{:S(2)}, u32[]{:S(2)}) collective-permute-start(bf16[256,512]{1,0:T(8,128)(2,1)S(1)} %constant_dynamic-slice_fusion.8), channel_id=1, source_target_pairs={{0,4},{2,6},{4,0},{6,2},{1,5},{3,7},{5,1},{7,3},{8,12},{10,14},{12... | collective-permute-start | bytes 786440 | tf_op jit(solution)/shard_map/ppermute | solution.py:190
  73.9 46.2 %collective-permute-start.18 = (bf16[256,512]{1,0:T(8,128)(2,1)S(1)}, bf16[256,512]{1,0:T(8,128)(2,1)S(1)}, u32[]{:S(2)}, u32[]{:S(2)}) collective-permute-start(bf16[256,512]{1,0:T(8,128)(2,1)S(1)} %constant_dynamic-slice_fusion.8), channel_id=1, source_target_pairs={{0,2},{2,4},{4,6},{6,0},{1,3},{3,5},{5,7},{7,1},{8,10},{10,12},{12... | collective-permute-start | bytes 786440 | tf_op jit(solution)/shard_map/ppermute | solution.py:190
  83.7 31.4 %collective-permute-start.14 = (bf16[96,2560]{1,0:T(8,128)(2,1)S(1)}, bf16[96,2560]{1,0:T(8,128)(2,1)S(1)}, u32[]{:S(2)}, u32[]{:S(2)}) collective-permute-start(bf16[96,2560]{1,0:T(8,128)(2,1)S(1)} %slice.257), channel_id=1, source_target_pairs={{0,8},{8,0},{16,24},{24,16},{1,9},{9,1},{17,25},{25,17},{2,10},{10... | collective-permute-start | bytes 1474568 | tf_op jit(solution)/shard_map/ppermute | solution.py:185
  85.3 29.9 %collective-permute-start.15 = (bf16[96,2560]{1,0:T(8,128)(2,1)S(1)}, bf16[96,2560]{1,0:T(8,128)(2,1)S(1)}, u32[]{:S(2)}, u32[]{:S(2)}) collective-permute-start(bf16[96,2560]{1,0:T(8,128)(2,1)S(1)} %slice.258), channel_id=1, source_target_pairs={{0,16},{8,24},{16,0},{24,8},{1,17},{9,25},{17,1},{25,9},{2,18},{10... | collective-permute-start | bytes 1474568 | tf_op jit(solution)/shard_map/ppermute | solution.py:185
  115.1 26.4 %collective-permute-start.8 = (bf16[1024,512]{1,0:T(8,128)(2,1)}, bf16[1024,512]{1,0:T(8,128)(2,1)}, u32[]{:S(2)}, u32[]{:S(2)}) collective-permute-start(bf16[1024,512]{1,0:T(8,128)(2,1)} %get-tuple-element.63), channel_id=1, source_target_pairs={{0,1},{1,0},{2,3},{3,2},{4,5},{5,4},{6,7},{7,6},{8,9},{9,8},{10,11... | collective-permute-start | bytes 3145736 | tf_op jit(solution)/shard_map/ppermute | solution.py:174
  219.5 54.2 %collective-permute-start.29 = (bf16[1024,1024]{0,1:T(8,128)(2,1)}, bf16[1024,1024]{0,1:T(8,128)(2,1)}, u32[]{:S(2)}, u32[]{:S(2)}) collective-permute-start(bf16[1024,1024]{0,1:T(8,128)(2,1)} %convolution_convert_fusion.5), channel_id=1, source_target_pairs={{0,1},{1,0},{2,3},{3,2},{4,5},{5,4},{6,7},{7,6},{8,9},{9,8},{10,11... | collective-permute-start | bytes 6291464 | tf_op jit(solution)/shard_map/ppermute | solution.py:174
  221.5 26.3 %collective-permute-start.30 = (bf16[2,2,256,512]{3,2,0,1:T(8,128)(2,1)}, bf16[2,2,256,512]{3,2,0,1:T(8,128)(2,1)}, u32[]{:S(2)}, u32[]{:S(2)}) collective-permute-start(bf16[2,2,256,512]{3,2,0,1:T(8,128)(2,1)} %copy_bitcast_fusion.3), channel_id=1, source_target_pairs={{0,8},{8,0},{16,24},{24,16},{1,9},{9,1},{17,25},{25,17},{2,10},{10... | collective-permute-start | bytes 3145736 | tf_op jit(solution)/shard_map/ppermute | solution.py:185
  223.0 27.0 %collective-permute-start.31 = (bf16[2,2,256,512]{3,2,0,1:T(8,128)(2,1)}, bf16[2,2,256,512]{3,2,0,1:T(8,128)(2,1)}, u32[]{:S(2)}, u32[]{:S(2)}) collective-permute-start(bf16[2,2,256,512]{3,2,0,1:T(8,128)(2,1)} %copy_bitcast_fusion.2), channel_id=1, source_target_pairs={{0,16},{8,24},{16,0},{24,8},{1,17},{9,25},{17,1},{25,9},{2,18},{10... | collective-permute-start | bytes 3145736 | tf_op jit(solution)/shard_map/ppermute | solution.py:185
  227.0 42.6 %collective-permute-start.32 = (bf16[2,2,64,2048]{3,2,0,1:T(8,128)(2,1)}, bf16[2,2,64,2048]{3,2,0,1:T(8,128)(2,1)}, u32[]{:S(2)}, u32[]{:S(2)}) collective-permute-start(bf16[2,2,64,2048]{3,2,0,1:T(8,128)(2,1)} %copy_bitcast_fusion.1), channel_id=1, source_target_pairs={{0,8},{8,0},{16,24},{24,16},{1,9},{9,1},{17,25},{25,17},{2,10},{10... | collective-permute-start | bytes 3145736 | tf_op jit(solution)/shard_map/ppermute | solution.py:185
  228.1 43.6 %collective-permute-start.33 = (bf16[2,2,64,2048]{3,2,0,1:T(8,128)(2,1)}, bf16[2,2,64,2048]{3,2,0,1:T(8,128)(2,1)}, u32[]{:S(2)}, u32[]{:S(2)}) collective-permute-start(bf16[2,2,64,2048]{3,2,0,1:T(8,128)(2,1)} %copy_bitcast_fusion), channel_id=1, source_target_pairs={{0,16},{8,24},{16,0},{24,8},{1,17},{9,25},{17,1},{25,9},{2,18},{10... | collective-permute-start | bytes 3145736 | tf_op jit(solution)/shard_map/ppermute | solution.py:185
  293.9 24.8 %collective-permute-start.67 = (f32[40,128]{1,0:T(8,128)S(1)}, f32[40,128]{1,0:T(8,128)S(1)}, u32[]{:S(2)}, u32[]{:S(2)}) collective-permute-start(f32[40,128]{1,0:T(8,128)S(1)} %fusion.112), channel_id=1, source_target_pairs={{0,16},{8,24},{16,0},{24,8},{1,17},{9,25},{17,1},{25,9},{2,18},{10... | collective-permute-start | bytes 61448 | tf_op jit(solution)/shard_map/ppermute | solution.py:185
  325.4 32.8 %collective-permute-start.36 = (bf16[2,64,2048]{2,1,0:T(8,128)(2,1)S(1)}, bf16[2,64,2048]{2,1,0:T(8,128)(2,1)S(1)}, u32[]{:S(2)}, u32[]{:S(2)}) collective-permute-start(bf16[2,64,2048]{2,1,0:T(8,128)(2,1)S(1)} %copy-done.46), channel_id=1, source_target_pairs={{0,16},{8,24},{16,0},{24,8},{1,17},{9,25},{17,1},{25,9},{2,18},{10... | collective-permute-start | bytes 1572872 | tf_op jit(solution)/shard_map/ppermute | solution.py:185
  333.3 27.3 %collective-permute-start.37 = (bf16[2,64,2048]{2,1,0:T(8,128)(2,1)S(1)}, bf16[2,64,2048]{2,1,0:T(8,128)(2,1)S(1)}, u32[]{:S(2)}, u32[]{:S(2)}) collective-permute-start(bf16[2,64,2048]{2,1,0:T(8,128)(2,1)S(1)} %copy-done.45), channel_id=1, source_target_pairs={{0,8},{8,0},{16,24},{24,16},{1,9},{9,1},{17,25},{25,17},{2,10},{10... | collective-permute-start | bytes 1572872 | tf_op jit(solution)/shard_map/ppermute | solution.py:185
  335.5 40.4 %collective-permute-start.69 = (f32[40,128]{1,0:T(8,128)}, f32[40,128]{1,0:T(8,128)}, u32[]{:S(2)}, u32[]{:S(2)}) collective-permute-start(f32[40,128]{1,0:T(8,128)} %add.581), channel_id=1, source_target_pairs={{0,4},{2,6},{4,0},{6,2},{1,5},{3,7},{5,1},{7,3},{8,12},{10,14},{12... | collective-permute-start | bytes 61448 | tf_op jit(solution)/shard_map/ppermute | solution.py:185
  403.2 24.8 %collective-permute-start.72 = (bf16[64,2048]{1,0:T(8,128)(2,1)S(1)}, bf16[64,2048]{1,0:T(8,128)(2,1)S(1)}, u32[]{:S(2)}, u32[]{:S(2)}) collective-permute-start(bf16[64,2048]{1,0:T(8,128)(2,1)S(1)} %copy-done.61), channel_id=1, source_target_pairs={{0,6},{2,0},{4,2},{6,4},{1,7},{3,1},{5,3},{7,5},{8,14},{10,8},{12,... | collective-permute-start | bytes 786440 | tf_op jit(solution)/shard_map/ppermute | solution.py:190
  426.4 110.4 %collective-permute-start.43 = (bf16[1024,512]{0,1:T(8,128)(2,1)S(1)}, bf16[1024,512]{0,1:T(8,128)(2,1)S(1)}, u32[]{:S(2)}, u32[]{:S(2)}) collective-permute-start(bf16[1024,512]{0,1:T(8,128)(2,1)S(1)} %slice.280), channel_id=1, source_target_pairs={{0,1},{1,0},{2,3},{3,2},{4,5},{5,4},{6,7},{7,6},{8,9},{9,8},{10,11... | collective-permute-start | bytes 3145736 | tf_op jit(solution)/shard_map/ppermute | solution.py:174
  429.9 40.4 %collective-permute-start.44 = (bf16[2,2,64,1536]{3,2,0,1:T(8,128)(2,1)S(1)}, bf16[2,2,64,1536]{3,2,0,1:T(8,128)(2,1)S(1)}, u32[]{:S(2)}, u32[]{:S(2)}) collective-permute-start(bf16[2,2,64,1536]{3,2,0,1:T(8,128)(2,1)S(1)} %copy-done.44), channel_id=1, source_target_pairs={{0,8},{8,0},{16,24},{24,16},{1,9},{9,1},{17,25},{25,17},{2,10},{10... | collective-permute-start | bytes 2359304 | tf_op jit(solution)/shard_map/ppermute | solution.py:185
  462.2 25.9 %collective-permute-start.46 = (bf16[2,2,64,1536]{3,2,0,1:T(8,128)(2,1)S(1)}, bf16[2,2,64,1536]{3,2,0,1:T(8,128)(2,1)S(1)}, u32[]{:S(2)}, u32[]{:S(2)}) collective-permute-start(bf16[2,2,64,1536]{3,2,0,1:T(8,128)(2,1)S(1)} %copy-done.43), channel_id=1, source_target_pairs={{0,16},{8,24},{16,0},{24,8},{1,17},{9,25},{17,1},{25,9},{2,18},{10... | collective-permute-start | bytes 2359304 | tf_op jit(solution)/shard_map/ppermute | solution.py:185
  468.5 45.5 %collective-permute-start.76 = (bf16[256,512]{1,0:T(8,128)(2,1)S(1)}, bf16[256,512]{1,0:T(8,128)(2,1)S(1)}, u32[]{:S(2)}, u32[]{:S(2)}) collective-permute-start(bf16[256,512]{1,0:T(8,128)(2,1)S(1)} %fusion.58), channel_id=1, source_target_pairs={{0,8},{8,0},{16,24},{24,16},{1,9},{9,1},{17,25},{25,17},{2,10},{10... | collective-permute-start | bytes 786440 | tf_op jit(solution)/shard_map/ppermute | solution.py:185
  468.5 48.4 %collective-permute-start.77 = (bf16[256,512]{1,0:T(8,128)(2,1)S(1)}, bf16[256,512]{1,0:T(8,128)(2,1)S(1)}, u32[]{:S(2)}, u32[]{:S(2)}) collective-permute-start(bf16[256,512]{1,0:T(8,128)(2,1)S(1)} %fusion.58), channel_id=1, source_target_pairs={{0,16},{8,24},{16,0},{24,8},{1,17},{9,25},{17,1},{25,9},{2,18},{10... | collective-permute-start | bytes 786440 | tf_op jit(solution)/shard_map/ppermute | solution.py:185
  470.5 32.5 %collective-permute-start.45 = (bf16[2,64,1536]{2,1,0:T(8,128)(2,1)S(1)}, bf16[2,64,1536]{2,1,0:T(8,128)(2,1)S(1)}, u32[]{:S(2)}, u32[]{:S(2)}) collective-permute-start(bf16[2,64,1536]{2,1,0:T(8,128)(2,1)S(1)} %fusion.50), channel_id=1, source_target_pairs={{0,16},{8,24},{16,0},{24,8},{1,17},{9,25},{17,1},{25,9},{2,18},{10... | collective-permute-start | bytes 1179656 | tf_op jit(solution)/shard_map/ppermute | solution.py:185
  488.1 30.8 %collective-permute-start.78 = (bf16[256,512]{1,0:T(8,128)(2,1)S(1)}, bf16[256,512]{1,0:T(8,128)(2,1)S(1)}, u32[]{:S(2)}, u32[]{:S(2)}) collective-permute-start(bf16[256,512]{1,0:T(8,128)(2,1)S(1)} %fusion.58), channel_id=1, source_target_pairs={{0,24},{8,16},{16,8},{24,0},{1,25},{9,17},{17,9},{25,1},{2,26},{10... | collective-permute-start | bytes 786440 | tf_op jit(solution)/shard_map/ppermute | solution.py:185
  (131 other events, 2040.6 us)
